TPU v7x, 32 devices: a whole 2x2x4 slice. The times are simulated.
32 devices in a mesh: tiles: 8 (over y, x, core), nodes: 4 (over z).
Axes of the slice: x: 2, y: 2, z: 4, core: 2. Of those that a mesh axis runs over, the one named last changes fastest.
Arguments:
- images: bfloat16 [512, 128, 128], P(('tiles', 'nodes')), may hold values from -6 to 6
- direction: float32 [4096, 3, 128], P(('tiles', 'nodes')), may hold values from -6 to 6
- damping: float32 [4096, 3, 128], P(('tiles', 'nodes')), may hold values from 0.5 to 4
- calibration: float32 [4, 2, 3], replicated, may hold values from -3 to 3
- camera: int32 [512], P(('tiles', 'nodes')), may hold values from 0 to 3
- owners: int32 [512, 16], P(('tiles', 'nodes')), may hold values from 0 to 31, all different within a row; in each aligned block of 16 rows (0 to 15, 16 to 31, ...) at most 16 rows name the same one
- local_block: int32 [512, 16], P(('tiles', 'nodes')), may hold values from 0 to 127
- connect: int32 [512, 4, 1024], P(('tiles', 'nodes')), may hold values from 0 to 2047
Outputs:
- product: float32 [4096, 3, 128], P(('tiles', 'nodes'))
Inputs may be any that keep to these rules, and one draw needn't show every extreme that they name: Within the rows of one device (aligned blocks of 16 tiles) each owner is named by at most 16 tiles, and exactly 16 in some block; a tile names 16 different owners.
All inputs are finite; a program needn't handle non-finite values.
Results may differ from a plain program's by a relative error of at most 0.0003.
Values sent between devices are 32-bit elements; how exact they have to be, the bound alone decides.
No kernel may reach another device: no remote copies, remote signals or barrier semaphores. Data moves between devices by JAX's collectives and lax.ppermute only.
A program may use at most 256 MiB of HBM per device.

v0:
```python
import jax
import jax.numpy as jnp
from jax import lax
from jax.sharding import PartitionSpec as P

EPX = 4


group_tiles = 8


def shape_table():
    position = (jnp.arange(EPX, dtype=jnp.float32) + 0.5) / EPX
    across = position[None, :]
    downward = position[:, None]
    return jnp.stack(
        [
            (1.0 - across) * (1.0 - downward),
            across * (1.0 - downward),
            (1.0 - across) * downward,
            across * downward,
        ]
    )


def slopes(pixels):
    slope_x = jnp.concatenate(
        [
            pixels[:, :, 1:2] - pixels[:, :, 0:1],
            0.5 * (pixels[:, :, 2:] - pixels[:, :, :-2]),
            pixels[:, :, -1:] - pixels[:, :, -2:-1],
        ],
        axis=2,
    )
    slope_y = jnp.concatenate(
        [
            pixels[:, 1:2, :] - pixels[:, 0:1, :],
            0.5 * (pixels[:, 2:, :] - pixels[:, :-2, :]),
            pixels[:, -1:, :] - pixels[:, -2:-1, :],
        ],
        axis=1,
    )
    return (slope_x, slope_y)


def to_elements(plane):
    tile_count = plane.shape[0]
    side_cells = plane.shape[1] // EPX
    return (
        plane.reshape(tile_count, side_cells, EPX, side_cells, EPX)
        .transpose(0, 2, 4, 1, 3)
        .reshape(tile_count, EPX, EPX, side_cells * side_cells)
    )


def tile_terms(
    slope_x, slope_y, projection, nodal_values, link_ids, weights, list_length, block_width
):
    group_count = nodal_values.shape[0]
    elem_count = link_ids.shape[2]
    values = nodal_values.reshape(group_count, 3 * list_length, block_width)
    block_of = link_ids // block_width
    node_of = link_ids - block_of * block_width
    node_range = jnp.arange(block_width, dtype=jnp.int32)[None, :, None]
    block_range = jnp.arange(list_length, dtype=jnp.int32)[None, :, None]
    node_tables = []
    block_tables = []
    picked_corners = []
    for corner in range(4):
        node_hot = (node_of[:, corner, None, :] == node_range).astype(jnp.float32)
        block_hot = (block_of[:, corner, None, :] == block_range).astype(jnp.float32)
        node_tables.append(node_hot)
        block_tables.append(block_hot)
        picked = jnp.einsum(
            "grn,gne->gre", values, node_hot, precision=lax.Precision.HIGHEST
        ).reshape(group_count, 3, list_length, elem_count)
        picked_corners.append(jnp.sum(picked * block_hot[:, None], axis=2))
    displaced = picked_corners[0][:, :, None, None, :] * weights[0][None, None, :, :, None]
    for corner in range(1, 4):
        displaced = (
            displaced
            + picked_corners[corner][:, :, None, None, :] * weights[corner][None, None, :, :, None]
        )

    def image_motion(motion_axis):
        result = projection[:, motion_axis, 0, None, None, None] * displaced[:, 0]
        result = result + projection[:, motion_axis, 1, None, None, None] * displaced[:, 1]
        return result + projection[:, motion_axis, 2, None, None, None] * displaced[:, 2]

    change = slope_x * image_motion(0) + slope_y * image_motion(1)
    force_x = slope_x * change
    force_y = slope_y * change
    pushed = jnp.stack(
        [
            projection[:, 0, component, None, None, None] * force_x
            + projection[:, 1, component, None, None, None] * force_y
            for component in range(3)
        ],
        axis=1,
    )
    gathered = jnp.sum(pushed[:, :, None] * weights[None, None, :, :, :, None], axis=(3, 4))
    summed = jnp.zeros((group_count, 3 * list_length, block_width), jnp.float32)
    for corner in range(4):
        spread = (gathered[:, :, corner, None, :] * block_tables[corner][:, None]).reshape(
            group_count, 3 * list_length, elem_count
        )
        summed = summed + jnp.einsum(
            "gre,gne->grn", spread, node_tables[corner], precision=lax.Precision.HIGHEST
        )
    return summed.reshape(group_count, 3, list_length * block_width)


def per_device(images, direction, damping, calibration, camera, owners, local_block, connect):
    device_count = lax.axis_size(("tiles", "nodes"))
    tiles_here = owners.shape[0]
    list_length = owners.shape[1]
    block_count = direction.shape[0]
    block_width = direction.shape[2]
    capacity = max(2, min(tiles_here, 4 * tiles_here * list_length // device_count))
    request_count = tiles_here * list_length
    flat_owner = owners.reshape(request_count)
    flat_local = local_block.reshape(request_count)
    owner_hits = (flat_owner[:, None] == jnp.arange(device_count, dtype=jnp.int32)[None, :]).astype(
        jnp.bfloat16
    )
    order_ids = jnp.arange(request_count, dtype=jnp.int32)
    earlier = (order_ids[:, None] > order_ids[None, :]).astype(jnp.bfloat16)
    before = jnp.dot(earlier, owner_hits, preferred_element_type=jnp.float32)
    ranked = jnp.sum(before * owner_hits.astype(jnp.float32), axis=1).astype(jnp.int32)
    slot_index = flat_owner * capacity + ranked
    wanted = (
        jnp.full((device_count * capacity,), -1, jnp.int32)
        .at[slot_index]
        .set(flat_local)
        .reshape(device_count, capacity)
    )
    asked_ids = lax.all_to_all(wanted, ("tiles", "nodes"), split_axis=0, concat_axis=0, tiled=True)
    weights = shape_table()
    as_float = images.astype(jnp.float32)
    slope_x, slope_y = slopes(as_float)
    slope_x = to_elements(slope_x)
    slope_y = to_elements(slope_y)
    projection = calibration[camera]
    served = asked_ids >= 0
    safe_ids = jnp.where(served, asked_ids, 0)
    outgoing = jnp.where(served[:, :, None, None], direction[safe_ids], 0.0)
    arrived = lax.all_to_all(outgoing, ("tiles", "nodes"), split_axis=0, concat_axis=0, tiled=True)
    fetched = arrived.reshape(device_count * capacity, 3, block_width)[slot_index]
    nodal_values = (
        fetched.reshape(tiles_here, list_length, 3, block_width)
        .transpose(0, 2, 1, 3)
        .reshape(tiles_here, 3, list_length * block_width)
    )
    groups = tiles_here // group_tiles

    def one_group(inputs):
        return tile_terms(
            inputs[0], inputs[1], inputs[2], inputs[3], inputs[4], weights, list_length, block_width
        )

    inputs = (
        slope_x.reshape(groups, group_tiles, EPX, EPX, -1),
        slope_y.reshape(groups, group_tiles, EPX, EPX, -1),
        projection.reshape(groups, group_tiles, 2, 3),
        nodal_values.reshape(groups, group_tiles, 3, -1),
        connect.reshape(groups, group_tiles, 4, -1),
    )
    partial_sums = lax.map(one_group, inputs)
    partial_sums = (
        partial_sums.reshape(tiles_here, 3, list_length, block_width)
        .transpose(0, 2, 1, 3)
        .reshape(request_count, 3, block_width)
    )
    global_ids = flat_owner * block_count + flat_local
    dense_sums = (
        jnp.zeros((device_count * block_count, 3, block_width), jnp.float32)
        .at[global_ids]
        .add(partial_sums)
    )
    node_sums = lax.psum_scatter(dense_sums, ("tiles", "nodes"), scatter_dimension=0, tiled=True)
    return node_sums + damping * direction


def solution(mesh):
    in_specs = (
        P(("tiles", "nodes"), None, None),
        P(("tiles", "nodes"), None, None),
        P(("tiles", "nodes"), None, None),
        P(),
        P(("tiles", "nodes")),
        P(("tiles", "nodes"), None),
        P(("tiles", "nodes"), None),
        P(("tiles", "nodes"), None, None),
    )
    out_specs = P(("tiles", "nodes"), None, None)
    return jax.shard_map(
        per_device, mesh=mesh, in_specs=in_specs, out_specs=out_specs, check_vma=False
    )
```

profile of v0, /device:TPU:1, one launch (start us, length us, event | category | flops | bytes accessed | tf_op | source)
XLA Modules:
  0.0 337.0 jit_solution(11458709399732777289)
XLA Ops:
  11.2 7.1 %all-to-all-start = ((s32[32,1,16]{2,1,0:T(1,128)}), s32[32,1,16]{2,1,0:T(1,128)S(1)}, u32[]{:S(2)}, u32[]{:S(2)}) async-start(s32[32,1,16]{2,1,0:T(1,128)} %bitcast.6), calls=%async_computation | async-start | bytes 32768 | tf_op jit(solution)/shard_map/all_to_all | solution.py:137
  21.3 4.6 %copy.180 = f32[16,128,128]{0,2,1:T(8,128)} copy(f32[16,128,128]{2,1,0:T(8,128)S(1)} %pad_maximum_fusion.1) | data formatting | bytes 2097152 | tf_op jit(solution)/shard_map/concatenate | solution.py:27
  26.0 8.7 %copy.181 = f32[16,4,4,32,32]{4,3,0,2,1:T(8,128)} copy(f32[16,4,4,32,32]{0,2,4,1,3:T(4,128)} %bitcast.165) | data formatting | bytes 2097152 | tf_op jit(solution)/shard_map/transpose | solution.py:51
  34.6 3.8 %reshape_reshape.9 = f32[2,8,4,4,1024]{4,1,0,3,2:T(8,128)S(1)} reshape(f32[16,4,4,32,32]{4,3,0,2,1:T(8,128)} %copy.181) | data formatting | bytes 2097152 | tf_op jit(solution)/shard_map/reshape;reshape | solution.py:162
  38.7 2.3 gather_fusion.1
  42.0 5.9 %all-to-all-start.1 = ((f32[32,16,3,128]{3,1,2,0:T(8,128)}), f32[32,16,3,128]{3,1,2,0:T(8,128)}, u32[]{:S(2)}, u32[]{:S(2)}) async-start(f32[32,16,3,128]{3,1,2,0:T(8,128)} %copy_select_fusion), calls=%async_computation.1 | async-start | bytes 1572864 | tf_op jit(solution)/shard_map/all_to_all | solution.py:147
  48.2 4.6 %copy.189 = f32[16,128,128]{0,2,1:T(8,128)} copy(f32[16,128,128]{2,1,0:T(8,128)S(1)} %pad_maximum_fusion.2) | data formatting | bytes 2097152 | tf_op jit(solution)/shard_map/concatenate | solution.py:35
  52.9 8.7 %copy.190 = f32[16,4,4,32,32]{4,3,0,2,1:T(8,128)} copy(f32[16,4,4,32,32]{0,2,4,1,3:T(4,128)} %bitcast.166) | data formatting | bytes 2097152 | tf_op jit(solution)/shard_map/transpose | solution.py:51
  61.6 3.8 %reshape_reshape.11 = f32[2,8,4,4,1024]{4,1,0,3,2:T(8,128)S(1)} reshape(f32[16,4,4,32,32]{4,3,0,2,1:T(8,128)} %copy.190) | data formatting | bytes 2097152 | tf_op jit(solution)/shard_map/reshape;reshape | solution.py:163
  66.3 2.5 all-to-all-done.1
  68.8 1.6 copy.186
  70.4 1.7 gather_fusion.2
  74.0 47.0 %while.14 = (s32[]{:T(128)}, f32[2,8,3,2048]{3,2,1,0:T(4,128)}, f32[2,8,2,3]{1,2,3,0:T(2,128)S(1)}, f32[2,8,4,4,1024]{4,1,0,3,2:T(8,128)S(1)}, f32[2,8,3,2048]{3...) while((s32[]{:T(128)}, f32[2,8,3,2048]{3,2,1,0:T(4,128)}, ...), condition=%wide.region_8.9_spmd.clone.clone, body=%wide.region_2.8_spmd.clone.clone.sunk | while | flops 4856332288 | bytes 53742044 | solution.py:168
  85.9 2.5 fusion.86
  88.9 2.5 fusion.85
  91.4 2.5 fusion.87
  94.2 2.5 fusion.88
  109.3 2.5 fusion.86
  112.4 2.5 fusion.85
  114.9 2.5 fusion.87
  117.6 2.5 fusion.88
  122.6 3.9 %broadcast_in_dim.28 = f32[4096,3,128]{2,1,0:T(4,128)} broadcast(f32[]{:T(128)} %constant.80.clone.1), dimensions={} | broadcast | bytes 6291460 | tf_op jit(solution)/shard_map/broadcast_in_dim | solution.py:176
  126.5 24.9 %scatter_fusion = f32[4096,3,128]{2,1,0:T(4,128)} fusion(f32[4096,3,128]{2,1,0:T(4,128)} %broadcast_in_dim.28, s32[256]{0:T(256)S(1)} %bitcast.177, f32[256,3,128]{2,1,0:T(4,128)S(1)} %copy.197), kind=kCustom, calls=%fused_computation.4 | custom fusion | flops 98304 | bytes 1180672 | tf_op jit(solution)/shard_map/scatter-add | solution.py:178
  151.4 177.0 %all-reduce.3.cloned.1.call-done = f32[4096,3,128]{2,1,0:T(4,128)} async-done(((f32[4096,3,128]{2,1,0:T(4,128)}), f32[4096,3,128]{2,1,0:T(4,128)}) %all-reduce.3.cloned.1.call-update) | async-done | bytes 6291472
  (137 shorter events, 42.0 us)
Async XLA Ops:
  11.2 27.2 %all-to-all-start = ((s32[32,1,16]{2,1,0:T(1,128)}), s32[32,1,16]{2,1,0:T(1,128)S(1)}, u32[]{:S(2)}, u32[]{:S(2)}) async-start(s32[32,1,16]{2,1,0:T(1,128)} %bitcast.6), calls=%async_computation | async-start | bytes 32768 | tf_op jit(solution)/shard_map/all_to_all | solution.py:137
  34.6 4.1 %copy-start = (f32[128,3,128]{2,0,1:T(8,128)S(1)}, f32[128,3,128]{2,0,1:T(8,128)}, u32[]{:S(2)}) copy-start(f32[128,3,128]{2,0,1:T(8,128)} %param.11) | copy-start | bytes 589828
  42.0 26.8 %all-to-all-start.1 = ((f32[32,16,3,128]{3,1,2,0:T(8,128)}), f32[32,16,3,128]{3,1,2,0:T(8,128)}, u32[]{:S(2)}, u32[]{:S(2)}) async-start(f32[32,16,3,128]{3,1,2,0:T(8,128)} %copy_select_fusion), calls=%async_computation.1 | async-start | bytes 1572864 | tf_op jit(solution)/shard_map/all_to_all | solution.py:147
  47.9 280.5 %all-reduce.3.cloned.1.call-start = ((), (), s32[]{:S(2)}) async-start(), calls=%async_computation.2 | async-start | bytes 16777216
  61.5 3.8 %copy-start.3 = (f32[4,2,3]{0,1,2:T(2,128)S(1)}, f32[4,2,3]{0,1,2:T(2,128)}, u32[]{:S(2)}) copy-start(f32[4,2,3]{0,1,2:T(2,128)} %param.13) | copy-start | bytes 292
  61.5 3.9 %copy-start.4 = (s32[16]{0:T(128)S(1)}, s32[16]{0:T(128)}, u32[]{:S(2)}) copy-start(s32[16]{0:T(128)} %param.14) | copy-start | bytes 196
  72.1 1.9 copy-start.1
  151.4 178.0 %copy-start.2 = (f32[128,3,128]{2,0,1:T(8,128)S(1)}, f32[128,3,128]{2,0,1:T(8,128)}, u32[]{:S(2)}) copy-start(f32[128,3,128]{2,0,1:T(8,128)} %param.12) | copy-start | bytes 589828
Sparse Core Ops, SparseCore 0:
  151.6 176.8 all-reduce.2
where the time goes:
time: 339 us; the launch traced here: 337 us
  waiting for transfers between devices  179 us (53%)
  local copies, waits for them, and re-layouts  58.3 us (17%)
  other arithmetic  40.2 us (12%)
  matrix products  31.8 us (9%)
  between operations  13.6 us (4%)
  starting transfers between devices  13 us (4%)
    unnamed x2, waiting for transfers between devices  177 us
    scatter-add x1, other arithmetic, per_device(): dense_sums = jnp.zeros((device_count * block_count, 3, block_width), jnp....  24.9 us
    dot_general x8, matrix products, tile_terms(): jnp.einsum('gre,gne->grn', spread, node_tables[corner], precision=lax.Pre...  19.8 us
    transpose x2, local copies, waits for them, and re-layouts, to_elements(): return plane.reshape(tile_count, side_cells, EPX, side_cells, EPX).transp...  17.3 us
    dot_general x8, matrix products, tile_terms(): jnp.einsum('grn,gne->gre', values, node_hot, precision=lax.Precision.HIGH...  11.7 us
    all_to_all x1, starting transfers between devices, per_device(): lax.all_to_all(wanted, ('tiles', 'nodes'), split_axis=0, concat_axis=0, t...  7.1 us
  transfers between devices with their start and end apart: 3, of which 2 were waited for; matrix products, arithmetic and copies ran while one was open for 11% of the time, Pallas kernels for 0%

commit v1 on v0

v1 whole, which is shorter than its diff:
```python
import functools

import jax
import jax.numpy as jnp
import numpy as np
from jax import lax
from jax.experimental import pallas as pl
from jax.experimental.pallas import tpu as pltpu
from jax.sharding import PartitionSpec as P

EPX = 4
LANES = 128
SUBS = 8
AXES = ("tiles", "nodes")
VMEM_LIMIT = 48 * 1024 * 1024


def pair_weights():
    x = (np.arange(EPX, dtype=np.float64) + 0.5) / EPX
    return np.stack([(1 - x) ** 2, x * (1 - x), x**2])


def column_pool(width):
    cells = width // EPX
    groups = LANES // cells
    weights = pair_weights()
    table = np.zeros((groups, width, 3, groups, cells), np.float32)
    for group in range(groups):
        for pixel in range(width):
            table[group, pixel, :, group, pixel // EPX] = weights[:, pixel % EPX]
    return table.reshape(groups * width, 3 * LANES)


def pixel_kernel(images_ref, pool_ref, out_ref, padded, pooled, *, tiles_step, groups):
    weights = pair_weights()
    height = images_ref.shape[1]
    width = images_ref.shape[2]
    stride = EPX * groups
    lane = lax.broadcasted_iota(jnp.int32, (SUBS, width), 1)
    first = lane == 0
    last = lane == width - 1
    scale = jnp.where(first | last, 1.0, 0.5).astype(jnp.float32)
    for tile in range(tiles_step):
        pixels = images_ref[tile].astype(jnp.float32)
        padded[pl.ds(SUBS, height), :] = pixels
        padded[pl.ds(SUBS - 1, 1), :] = 2.0 * pixels[0:1] - pixels[1:2]
        padded[pl.ds(SUBS + height, 1), :] = 2.0 * pixels[height - 1 :] - pixels[height - 2 : height - 1]
        for group in range(groups):
            sums = [[None] * 3 for _ in range(3)]
            rows = [
                padded[pl.ds(SUBS + group * EPX + step, SUBS, stride=stride), :]
                for step in range(-1, EPX + 1)
            ]
            for step in range(EPX):
                here = rows[step + 1]
                slope_y = 0.5 * (rows[step + 2] - rows[step])
                left = jnp.where(first, here, pltpu.roll(here, 1, 1))
                right = jnp.where(last, here, pltpu.roll(here, width - 1, 1))
                slope_x = scale * (right - left)
                products = (slope_x * slope_x, slope_x * slope_y, slope_y * slope_y)
                for kind in range(3):
                    for pair in range(3):
                        term = float(weights[pair, step]) * products[kind]
                        old = sums[kind][pair]
                        sums[kind][pair] = term if old is None else old + term
            for kind in range(3):
                for pair in range(3):
                    row = (tile * 9 + kind * 3 + pair) * SUBS
                    pooled[pl.ds(row, SUBS), pl.ds(group * width, width)] = sums[kind][pair]
    values = pooled[...]
    high = values.astype(jnp.bfloat16)
    low = (values - high.astype(jnp.float32)).astype(jnp.bfloat16)
    pool = pool_ref[...]
    out_ref[...] = jnp.dot(high, pool, preferred_element_type=jnp.float32) + jnp.dot(
        low, pool, preferred_element_type=jnp.float32
    )


def pixel_sums(images):
    tiles, height, width = images.shape
    groups = LANES * EPX // width
    tiles_step = 4
    rows = tiles_step * 9 * SUBS
    pool = jnp.asarray(column_pool(width), jnp.bfloat16)
    return pl.pallas_call(
        functools.partial(pixel_kernel, tiles_step=tiles_step, groups=groups),
        grid=(tiles // tiles_step,),
        in_specs=[
            pl.BlockSpec((tiles_step, height, width), lambda i: (i, 0, 0)),
            pl.BlockSpec(pool.shape, lambda i: (0, 0)),
        ],
        out_specs=pl.BlockSpec((rows, 3 * LANES), lambda i: (i, 0)),
        out_shape=jax.ShapeDtypeStruct((tiles * 9 * SUBS, 3 * LANES), jnp.float32),
        scratch_shapes=[
            pltpu.VMEM((height + 2 * SUBS, width), jnp.float32),
            pltpu.VMEM((rows, groups * width), jnp.float32),
        ],
        compiler_params=pltpu.CompilerParams(vmem_limit_bytes=VMEM_LIMIT),
        cost_estimate=pl.CostEstimate(
            flops=tiles * 2 * 72 * 512 * 384 * 4, bytes_accessed=4 * images.size, transcendentals=0
        ),
        name="pixel_sums",
    )(images, pool)


def serve_kernel(codes_ref, calibration_ref, direction_ref, out_ref, table, *, capacity, devices):
    blocks = direction_ref.shape[1]
    cameras = calibration_ref.shape[0] // 6
    parts = [direction_ref[axis] for axis in range(3)]
    for camera in range(cameras):
        for motion in range(2):
            base = camera * 6 + motion * 3
            seen = calibration_ref[base] * parts[0]
            seen = seen + calibration_ref[base + 1] * parts[1]
            seen = seen + calibration_ref[base + 2] * parts[2]
            table[pl.ds((motion * cameras + camera) * blocks, blocks), :] = seen

    def one_device(device, carry):
        for slot in range(capacity):
            code = jnp.maximum(codes_ref[device * capacity + slot], 0)
            for motion in range(2):
                row = device * (2 * capacity) + motion * capacity + slot
                out_ref[pl.ds(row, 1), :] = table[pl.ds(motion * cameras * blocks + code, 1), :]
        return carry

    lax.fori_loop(0, devices, one_device, 0)


def serve(codes, calibration, direction, capacity, devices):
    _, blocks, width = direction.shape
    cameras = calibration.shape[0]
    return pl.pallas_call(
        functools.partial(serve_kernel, capacity=capacity, devices=devices),
        in_specs=[
            pl.BlockSpec(memory_space=pltpu.SMEM),
            pl.BlockSpec(memory_space=pltpu.SMEM),
            pl.BlockSpec(memory_space=pltpu.VMEM),
        ],
        out_specs=pl.BlockSpec(memory_space=pltpu.VMEM),
        out_shape=jax.ShapeDtypeStruct((devices * 2 * capacity, width), jnp.float32),
        scratch_shapes=[pltpu.VMEM((2 * cameras * blocks, width), jnp.float32)],
        compiler_params=pltpu.CompilerParams(vmem_limit_bytes=VMEM_LIMIT),
        name="serve",
    )(codes, calibration.reshape(-1), direction)


def tile_kernel(place_ref, arrived_ref, sums_ref, connect_ref, out_ref, result, *, capacity, listed):
    tile = pl.program_id(0)

    @pl.when(tile == 0)
    def _():
        out_ref[...] = jnp.zeros_like(out_ref)

    shape = (SUBS, LANES)
    node_of = []
    block_of = []
    motion = [[jnp.zeros(shape, jnp.float32) for _ in range(2)] for _ in range(4)]
    for corner in range(4):
        link = connect_ref[0, corner]
        node_of.append(jnp.bitwise_and(link, LANES - 1))
        block_of.append(jnp.right_shift(link, 7))
    for entry in range(listed):
        place = place_ref[tile * listed + entry]
        rows = [
            jnp.broadcast_to(arrived_ref[pl.ds(place + axis * capacity, 1), :], shape) for axis in range(2)
        ]
        for corner in range(4):
            here = block_of[corner] == entry
            for axis in range(2):
                picked = jnp.take_along_axis(rows[axis], node_of[corner], axis=1, mode="promise_in_bounds")
                motion[corner][axis] = jnp.where(here, picked, motion[corner][axis])

    def element(kind, pair_y, pair_x):
        return sums_ref[pl.ds((kind * 3 + pair_y) * SUBS, SUBS), pl.ds(pair_x * LANES, LANES)]

    forces = []
    for corner in range(4):
        both = []
        for axis in range(2):
            total = None
            for other in range(4):
                pair_x = corner % 2 + other % 2
                pair_y = corner // 2 + other // 2
                for source in range(2):
                    term = element(axis + source, pair_y, pair_x) * motion[other][source]
                    total = term if total is None else total + term
            both.append(total)
        forces.append(both)

    node_ids = lax.broadcasted_iota(jnp.int32, (LANES, LANES), 0)
    block_ids = lax.broadcasted_iota(jnp.int32, (listed, LANES), 0)
    total = jnp.zeros((4 * listed, LANES), jnp.float32)
    for corner in range(4):
        hots = []
        spreads = []
        split = []
        for axis in range(2):
            high = forces[corner][axis].astype(jnp.bfloat16).astype(jnp.float32)
            split += [high, forces[corner][axis] - high]
        for chunk in range(SUBS):
            nodes = jnp.broadcast_to(node_of[corner][chunk : chunk + 1], (LANES, LANES))
            hots.append(jnp.where(nodes == node_ids, 1.0, 0.0).astype(jnp.bfloat16))
            here = jnp.broadcast_to(block_of[corner][chunk : chunk + 1], (listed, LANES)) == block_ids
            spreads.append(
                jnp.concatenate(
                    [
                        jnp.where(here, jnp.broadcast_to(part[chunk : chunk + 1], (listed, LANES)), 0.0).astype(
                            jnp.bfloat16
                        )
                        for part in split
                    ],
                    axis=0,
                )
            )
        hot = jnp.concatenate(hots, axis=1)
        spread = jnp.concatenate(spreads, axis=1)
        total = total + lax.dot_general(
            spread, hot, (((1,), (1,)), ((), ())), preferred_element_type=jnp.float32
        )
    for axis in range(2):
        base = 2 * axis * listed
        result[pl.ds(axis * listed, listed), :] = (
            total[base : base + listed] + total[base + listed : base + 2 * listed]
        )
    for entry in range(listed):
        place = place_ref[tile * listed + entry]
        for axis in range(2):
            out_ref[pl.ds(place + axis * capacity, 1), :] = result[pl.ds(axis * listed + entry, 1), :]


def tile_forces(places, arrived, sums, connect, capacity, listed):
    tiles = connect.shape[0]
    return pl.pallas_call(
        functools.partial(tile_kernel, capacity=capacity, listed=listed),
        grid_spec=pltpu.PrefetchScalarGridSpec(
            num_scalar_prefetch=1,
            grid=(tiles,),
            in_specs=[
                pl.BlockSpec(arrived.shape, lambda i, *_: (0, 0)),
                pl.BlockSpec((9 * SUBS, 3 * LANES), lambda i, *_: (i, 0)),
                pl.BlockSpec((1, 4, SUBS, LANES), lambda i, *_: (i, 0, 0, 0)),
            ],
            out_specs=pl.BlockSpec(arrived.shape, lambda i, *_: (0, 0)),
            scratch_shapes=[pltpu.VMEM((2 * listed, LANES), jnp.float32)],
        ),
        out_shape=jax.ShapeDtypeStruct(arrived.shape, jnp.float32),
        compiler_params=pltpu.CompilerParams(vmem_limit_bytes=VMEM_LIMIT),
        name="tile_forces",
    )(places, arrived, sums, connect)


def finish_kernel(calibration_ref, codes_ref, back_ref, direction_ref, damping_ref, out_ref, *, capacity, devices):
    blocks = direction_ref.shape[1]
    cameras = calibration_ref.shape[0] // 6
    slots = devices * capacity
    back = back_ref[...].reshape(devices, 2, capacity, LANES)
    halves = []
    for motion in range(2):
        values = back[:, motion].reshape(slots, LANES)
        high = values.astype(jnp.bfloat16)
        halves += [high, (values - high.astype(jnp.float32)).astype(jnp.bfloat16)]
    right = jnp.concatenate(halves, axis=1)
    ids = lax.broadcasted_iota(jnp.int32, (cameras * blocks, LANES), 0)
    hot = jnp.concatenate(
        [
            jnp.where(
                jnp.broadcast_to(codes_ref[pl.ds(part, 1), :], ids.shape) == ids, 1.0, 0.0
            ).astype(jnp.bfloat16)
            for part in range(slots // LANES)
        ],
        axis=1,
    )
    summed = jnp.dot(hot, right, preferred_element_type=jnp.float32)
    seen = [
        summed[:, 2 * motion * LANES : (2 * motion + 1) * LANES]
        + summed[:, (2 * motion + 1) * LANES : (2 * motion + 2) * LANES]
        for motion in range(2)
    ]
    for axis in range(3):
        total = damping_ref[axis] * direction_ref[axis]
        for camera in range(cameras):
            for motion in range(2):
                part = seen[motion][camera * blocks : (camera + 1) * blocks]
                total = total + calibration_ref[camera * 6 + motion * 3 + axis] * part
        out_ref[axis] = total


def finish(calibration, codes, back, direction, damping, capacity, devices):
    vmem = pl.BlockSpec(memory_space=pltpu.VMEM)
    return pl.pallas_call(
        functools.partial(finish_kernel, capacity=capacity, devices=devices),
        in_specs=[pl.BlockSpec(memory_space=pltpu.SMEM), vmem, vmem, vmem, vmem],
        out_specs=vmem,
        out_shape=jax.ShapeDtypeStruct(direction.shape, jnp.float32),
        compiler_params=pltpu.CompilerParams(vmem_limit_bytes=VMEM_LIMIT),
        name="finish",
    )(calibration.reshape(-1), codes, back, direction, damping)


def exchange(values):
    return lax.all_to_all(values, AXES, split_axis=0, concat_axis=0, tiled=True)


def per_device(images, direction, damping, calibration, camera, owners, local_block, connect):
    devices = lax.axis_size(AXES)
    tiles, listed = owners.shape
    blocks, _, width = direction.shape
    capacity = max(2, min(tiles, 4 * tiles * listed // devices))
    direction = direction.transpose(1, 0, 2)
    damping = damping.transpose(1, 0, 2)
    everyone = jnp.arange(devices, dtype=jnp.int32)
    code = camera[:, None] * blocks + local_block
    hits = owners[None, :, :] == everyone[:, None, None]
    named = jnp.sum(jnp.where(hits, code[None] + 1, 0), axis=2)
    if capacity == tiles:
        wanted = named - 1
        slot = jnp.broadcast_to(jnp.arange(tiles, dtype=jnp.int32)[:, None], owners.shape)
    else:
        taken = (named > 0).astype(jnp.int32)
        rank = jnp.cumsum(taken, axis=1) - taken
        slots = jnp.arange(capacity, dtype=jnp.int32)
        chosen = (rank[:, :, None] == slots[None, None, :]) & (taken[:, :, None] > 0)
        wanted = jnp.sum(jnp.where(chosen, named[:, :, None], 0), axis=1) - 1
        slot = jnp.sum(jnp.where(hits, rank[:, :, None], 0), axis=0)
    places = (owners * (2 * capacity) + slot).reshape(-1)
    asked = exchange(wanted).reshape(-1)
    sums = pixel_sums(images)
    outgoing = serve(asked, calibration, direction, capacity, devices)
    shape = (devices, 2 * capacity, width)
    arrived = exchange(outgoing.reshape(shape)).reshape(-1, width)
    forces = tile_forces(places, arrived, sums, connect.reshape(tiles, 4, SUBS, LANES), capacity, listed)
    back = exchange(forces.reshape(shape)).reshape(-1, width)
    product = finish(calibration, asked.reshape(-1, LANES), back, direction, damping, capacity, devices)
    return product.transpose(1, 0, 2)


def solution(mesh):
    split = P(AXES)
    return jax.shard_map(
        per_device,
        mesh=mesh,
        in_specs=(split, split, split, P(), split, split, split, split),
        out_specs=split,
        check_vma=False,
    )
```

time: 339 us -> 73.3 us (0.22)
  waiting for transfers between devices: 179 us -> 32.2 us
  local copies, waits for them, and re-layouts: 58.3 us -> 3.35 us
  other arithmetic: 40.2 us -> 2.98 us
  matrix products: 31.8 us -> 0 us
  Pallas kernels: 0 us -> 21 us
  between operations: 13.6 us -> 0.1 us
    unnamed x2 -> x0, waiting for transfers between devices: 177 us -> none
    dot_general x17 -> x0, matrix products: 31.8 us -> none  [the longest x8 19.8 us: tile_terms(): jnp.einsum('gre,gne->grn', spread, node_tables[corner], precision=lax.Pre...]
    all_to_all x2 -> x3, waiting for transfers between devices: 2.48 us -> 32.2 us  [exchange(): return lax.all_to_all(values, AXES, split_axis=0, concat_axis=0, tiled=True)]
    scatter-add x1 -> x0, other arithmetic: 24.9 us -> none  [per_device(): dense_sums = jnp.zeros((device_count * block_count, 3, block_width), jnp....]
    pallas_call x0 -> x4, Pallas kernels: none -> 21 us  [the longest x1 14.2 us: tile_forces(): pl.pallas_call(functools.partial(tile_kernel, capacity=capacity, listed=l...]
    transpose x2 -> x0, local copies, waits for them, and re-layouts: 17.3 us -> none  [to_elements(): return plane.reshape(tile_count, side_cells, EPX, side_cells, EPX).transp...]
    concatenate x2 -> x0, local copies, waits for them, and re-layouts: 9.26 us -> none  [the longest x1 4.63 us: slopes(): jnp.concatenate([pixels[:, :, 1:2] - pixels[:, :, 0:1], 0.5 * (pixels[:,...]
    another operation x3 -> x1, local copies, waits for them, and re-layouts: 8.36 us -> 0.08 us  [per_device(): asked.reshape(-1, LANES)]
  transfers between devices with their start and end apart: 3 -> 3, of which waited for: 2 -> 3; matrix products, arithmetic and copies ran while one was open for 11% -> 3% of each run, Pallas kernels for 0% -> 4%
where the time goes in v1:
time: 73.3 us; the launch traced here: 72.8 us
  waiting for transfers between devices  32.2 us (44%)
  Pallas kernels  21 us (29%)
  starting transfers between devices  13.2 us (18%)
  local copies, waits for them, and re-layouts  3.35 us (5%)
  other arithmetic  2.98 us (4%)
    all_to_all x3, waiting for transfers between devices, exchange(): return lax.all_to_all(values, AXES, split_axis=0, concat_axis=0, tiled=True)  32.2 us
    pallas_call x1, Pallas kernels, tile_forces(): pl.pallas_call(functools.partial(tile_kernel, capacity=capacity, listed=l...  14.2 us
    all_to_all x3, starting transfers between devices, exchange(): return lax.all_to_all(values, AXES, split_axis=0, concat_axis=0, tiled=True)  13.2 us
    pallas_call x1, Pallas kernels, pixel_sums(): pl.pallas_call(functools.partial(pixel_kernel, tiles_step=tiles_step, gro...  2.79 us
    pallas_call x1, Pallas kernels, serve(): pl.pallas_call(functools.partial(serve_kernel, capacity=capacity, devices...  2.33 us
    unnamed x15, local copies, waits for them, and re-layouts  1.73 us
    pallas_call x1, Pallas kernels, finish(): pl.pallas_call(functools.partial(finish_kernel, capacity=capacity, device...  1.67 us
  transfers between devices with their start and end apart: 3, of which 3 were waited for; matrix products, arithmetic and copies ran while one was open for 3% of the time, Pallas kernels for 4%

profile of v1, /device:TPU:1, one launch (start us, length us, event | category | flops | bytes accessed | tf_op | source)
XLA Modules:
  0.0 72.8 jit_solution(9991868994206408243)
XLA Ops:
  0.0 0.7 broadcast_multiply_fusion
  0.7 0.8 %add_add_fusion = s32[16,16]{1,0:T(8,128)S(1)} fusion(s32[16,16]{1,0:T(8,128)} %param.15, s32[16]{0:T(128)S(1)} %broadcast_multiply_fusion), kind=kLoop, calls=%fused_computation.4 | loop fusion | flops 512 | bytes 2112 | tf_op jit(solution)/shard_map/add | solution.py:314
  1.4 0.8 %select_reduce_fusion = s32[32,16]{0,1:T(8,128)S(1)} fusion(s32[16,16]{1,0:T(8,128)S(1)} %add_add_fusion, s32[16,16]{1,0:T(8,128)} %param.14), kind=kLoop, calls=%fused_computation | loop fusion | flops 24064 | bytes 4096 | tf_op jit(solution)/shard_map/reduce_sum | solution.py:314
  2.3 0.7 copy.14
  3.0 7.1 %all-to-all-start = ((s32[32,1,16]{2,1,0:T(1,128)}), s32[32,1,16]{2,1,0:T(1,128)S(1)}, u32[]{:S(2)}, u32[]{:S(2)}) async-start(s32[32,1,16]{2,1,0:T(1,128)} %copy.14), calls=%async_computation | async-start | bytes 32768 | tf_op jit(solution)/shard_map/all_to_all | solution.py:301
  10.1 0.8 %copy.13 = f32[4,2,3]{2,1,0:T(2,128)S(1)} copy(f32[4,2,3]{0,1,2:T(2,128)} %param.12) | data formatting | bytes 192 | tf_op args[3]
  10.9 0.1 reshape.43.calibration_ref
  11.0 5.7 %all-to-all-done = s32[32,1,16]{2,1,0:T(1,128)S(1)} async-done(((s32[32,1,16]{2,1,0:T(1,128)}), s32[32,1,16]{2,1,0:T(1,128)S(1)}, u32[]{:S(2)}, u32[]{:S(2)}) %all-to-all-start) | async-done | bytes 2080 | tf_op jit(solution)/shard_map/all_to_all | solution.py:301
  16.7 0.1 reshape.45.codes_ref
  16.8 0.9 %copy-done = f32[128,3,128]{2,0,1:T(8,128)S(1)} copy-done((f32[128,3,128]{2,0,1:T(8,128)S(1)}, f32[128,3,128]{2,0,1:T(8,128)}, u32[]{:S(2)}) %copy-start) | copy-done | bytes 196632
  17.7 2.3 %serve.1 = f32[1024,128]{1,0:T(8,128)} custom-call(s32[512]{0:T(512)S(1)} %reshape.45.codes_ref, f32[24]{0:T(128)S(1)} %reshape.43.calibration_ref, f32[3,128,128]{2,1,0:T(8,128)S(1)} %bitcast.12), custom_call_target="tpu_custom_call" | custom-call | tf_op jit(solution)/shard_map/serve/pallas_call | solution.py:132
  20.0 2.9 %all-to-all-start.1 = ((f32[32,32,128]{2,1,0:T(8,128)}), f32[32,32,128]{2,1,0:T(8,128)S(1)}, u32[]{:S(2)}, u32[]{:S(2)}) async-start(f32[32,32,128]{2,1,0:T(8,128)} %bitcast.2), calls=%async_computation.1 | async-start | bytes 1048576 | tf_op jit(solution)/shard_map/all_to_all | solution.py:301
  23.0 0.0 copy-done.6
  23.0 0.1 reshape.44.place_ref
  23.1 0.1 reshape.48.connect_ref
  23.2 2.8 %pixel_sums.1.sums_ref = f32[1152,384]{1,0:T(8,128)S(1)} custom-call(bf16[16,128,128]{2,1,0:T(8,128)(2,1)S(1)} %copy-done.3, bf16[512,384]{1,0:T(8,128)(2,1)S(1)} %copy-done.4), custom_call_target="tpu_custom_call" | custom-call | flops 1811939328 | bytes 1048576 | tf_op jit(solution)/shard_map/pixel_sums/pallas_call | solution.py:85
  26.0 12.4 %all-to-all-done.1 = f32[32,32,128]{2,1,0:T(8,128)S(1)} async-done(((f32[32,32,128]{2,1,0:T(8,128)}), f32[32,32,128]{2,1,0:T(8,128)S(1)}, u32[]{:S(2)}, u32[]{:S(2)}) %all-to-all-start.1) | async-done | bytes 524320 | tf_op jit(solution)/shard_map/all_to_all | solution.py:301
  38.4 14.2 %tile_forces.1 = f32[1024,128]{1,0:T(8,128)} custom-call(s32[256]{0:T(256)S(1)} %reshape.44.place_ref, f32[1024,128]{1,0:T(8,128)S(1)} %bitcast.11, f32[1152,384]{1,0:T(8,128)S(1)} %pixel_sums.1.sums_ref, s32[16,4,8,128]{3,2,1,0:T(8,128)S(1)} %reshape.48.connect_ref), custom_call_target="tpu_custom_call" | custom-call | tf_op jit(solution)/shard_map/tile_forces/pallas_call | solution.py:233
  52.7 3.1 %all-to-all-start.2 = ((f32[32,32,128]{2,1,0:T(8,128)}), f32[32,32,128]{2,1,0:T(8,128)S(1)}, u32[]{:S(2)}, u32[]{:S(2)}) async-start(f32[32,32,128]{2,1,0:T(8,128)} %bitcast.4), calls=%async_computation.2 | async-start | bytes 1048576 | tf_op jit(solution)/shard_map/all_to_all | solution.py:301
  55.8 0.5 broadcast.29
  56.3 0.7 reduce.5
  57.0 0.1 reshape_reshape.3.codes_ref
  57.1 14.0 %all-to-all-done.2 = f32[32,32,128]{2,1,0:T(8,128)S(1)} async-done(((f32[32,32,128]{2,1,0:T(8,128)}), f32[32,32,128]{2,1,0:T(8,128)S(1)}, u32[]{:S(2)}, u32[]{:S(2)}) %all-to-all-start.2) | async-done | bytes 524320 | tf_op jit(solution)/shard_map/all_to_all | solution.py:301
  71.1 1.7 %finish.1 = f32[3,128,128]{2,1,0:T(8,128)} custom-call(f32[24]{0:T(128)S(1)} %reshape.43.calibration_ref, s32[4,128]{1,0:T(4,128)S(1)} %reshape_reshape.3.codes_ref, f32[1024,128]{1,0:T(8,128)S(1)} %bitcast.10, f32[3,128,128]{2,1,0:T(8,128)S(1)} %bitcast.13, f32[3,128,128]{2,1,0:T(8,128)S(1)} %bitcast.14), custom_call_target="tpu_custom_call" | custom-call | tf_op jit(solution)/shard_map/finish/pallas_call | solution.py:290
  (14 shorter events, 0.0 us)
Async XLA Ops:
  0.0 23.0 %copy-start.6 = (s32[16,16]{1,0:T(8,128)S(1)}, s32[16,16]{1,0:T(8,128)}, u32[]{:S(2)}) copy-start(s32[16,16]{1,0:T(8,128)} %param.14) | copy-start | bytes 3076
  3.0 13.7 %all-to-all-start = ((s32[32,1,16]{2,1,0:T(1,128)}), s32[32,1,16]{2,1,0:T(1,128)S(1)}, u32[]{:S(2)}, u32[]{:S(2)}) async-start(s32[32,1,16]{2,1,0:T(1,128)} %copy.14), calls=%async_computation | async-start | bytes 32768 | tf_op jit(solution)/shard_map/all_to_all | solution.py:301
  16.8 0.9 %copy-start = (f32[128,3,128]{2,0,1:T(8,128)S(1)}, f32[128,3,128]{2,0,1:T(8,128)}, u32[]{:S(2)}) copy-start(f32[128,3,128]{2,0,1:T(8,128)} %param.10) | copy-start | bytes 589828
  17.7 5.4 %copy-start.5 = (s32[16,4,1024]{2,1,0:T(4,128)S(1)}, s32[16,4,1024]{2,1,0:T(4,128)}, u32[]{:S(2)}) copy-start(s32[16,4,1024]{2,1,0:T(4,128)} %param.16) | copy-start | bytes 786436
  17.7 5.5 %copy-start.3 = (bf16[16,128,128]{2,1,0:T(8,128)(2,1)S(1)}, bf16[16,128,128]{2,1,0:T(8,128)(2,1)}, u32[]{:S(2)}) copy-start(bf16[16,128,128]{2,1,0:T(8,128)(2,1)} %images_ref.1) | copy-start | bytes 1572868
  17.7 5.5 %copy-start.4 = (bf16[512,384]{1,0:T(8,128)(2,1)S(1)}, bf16[512,384]{1,0:T(8,128)(2,1)}, u32[]{:S(2)}) copy-start(bf16[512,384]{1,0:T(8,128)(2,1)} %constant.13.clone.pool_ref) | copy-start | bytes 1179652
  20.0 18.4 %all-to-all-start.1 = ((f32[32,32,128]{2,1,0:T(8,128)}), f32[32,32,128]{2,1,0:T(8,128)S(1)}, u32[]{:S(2)}, u32[]{:S(2)}) async-start(f32[32,32,128]{2,1,0:T(8,128)} %bitcast.2), calls=%async_computation.1 | async-start | bytes 1048576 | tf_op jit(solution)/shard_map/all_to_all | solution.py:301
  38.4 32.7 %copy-start.1 = (f32[128,3,128]{2,0,1:T(8,128)S(1)}, f32[128,3,128]{2,0,1:T(8,128)}, u32[]{:S(2)}) copy-start(f32[128,3,128]{2,0,1:T(8,128)} %param.10) | copy-start | bytes 589828
  38.4 32.7 %copy-start.2 = (f32[128,3,128]{2,0,1:T(8,128)S(1)}, f32[128,3,128]{2,0,1:T(8,128)}, u32[]{:S(2)}) copy-start(f32[128,3,128]{2,0,1:T(8,128)} %param.11) | copy-start | bytes 589828
  52.7 18.4 %all-to-all-start.2 = ((f32[32,32,128]{2,1,0:T(8,128)}), f32[32,32,128]{2,1,0:T(8,128)S(1)}, u32[]{:S(2)}, u32[]{:S(2)}) async-start(f32[32,32,128]{2,1,0:T(8,128)} %bitcast.4), calls=%async_computation.2 | async-start | bytes 1048576 | tf_op jit(solution)/shard_map/all_to_all | solution.py:301

commit v2 on v1

v2 whole, which is shorter than its diff:
```python
import functools
import math

import jax
import jax.numpy as jnp
import numpy as np
from jax import lax
from jax.experimental import pallas as pl
from jax.experimental.pallas import tpu as pltpu
from jax.sharding import PartitionSpec as P

EPX = 4
LANES = 128
SUBS = 8
AXES = ("tiles", "nodes")
VMEM_LIMIT = 48 * 1024 * 1024


def pair_weights():
    x = (np.arange(EPX, dtype=np.float64) + 0.5) / EPX
    return np.stack([(1 - x) ** 2, x * (1 - x), x**2])


def column_pool(width):
    cells = width // EPX
    groups = LANES // cells
    weights = pair_weights()
    table = np.zeros((groups, width, 3, groups, cells), np.float32)
    for group in range(groups):
        for pixel in range(width):
            table[group, pixel, :, group, pixel // EPX] = weights[:, pixel % EPX]
    return table.reshape(groups * width, 3 * LANES)


def pixel_kernel(images_ref, pool_ref, out_ref, padded, pooled, *, tiles_step, groups):
    weights = pair_weights()
    height = images_ref.shape[1]
    width = images_ref.shape[2]
    stride = EPX * groups
    lane = lax.broadcasted_iota(jnp.int32, (SUBS, width), 1)
    first = lane == 0
    last = lane == width - 1
    scale = jnp.where(first | last, 1.0, 0.5).astype(jnp.float32)
    for tile in range(tiles_step):
        pixels = images_ref[tile].astype(jnp.float32)
        padded[pl.ds(SUBS, height), :] = pixels
        padded[pl.ds(SUBS - 1, 1), :] = 2.0 * pixels[0:1] - pixels[1:2]
        padded[pl.ds(SUBS + height, 1), :] = 2.0 * pixels[height - 1 :] - pixels[height - 2 : height - 1]
        for group in range(groups):
            sums = [[None] * 3 for _ in range(3)]
            rows = [
                padded[pl.ds(SUBS + group * EPX + step, SUBS, stride=stride), :]
                for step in range(-1, EPX + 1)
            ]
            for step in range(EPX):
                here = rows[step + 1]
                slope_y = 0.5 * (rows[step + 2] - rows[step])
                left = jnp.where(first, here, pltpu.roll(here, 1, 1))
                right = jnp.where(last, here, pltpu.roll(here, width - 1, 1))
                slope_x = scale * (right - left)
                products = (slope_x * slope_x, slope_x * slope_y, slope_y * slope_y)
                for kind in range(3):
                    for pair in range(3):
                        term = float(weights[pair, step]) * products[kind]
                        old = sums[kind][pair]
                        sums[kind][pair] = term if old is None else old + term
            for kind in range(3):
                for pair in range(3):
                    row = (tile * 9 + kind * 3 + pair) * SUBS
                    pooled[pl.ds(row, SUBS), pl.ds(group * width, width)] = sums[kind][pair]
    values = pooled[...]
    high = values.astype(jnp.bfloat16)
    low = (values - high.astype(jnp.float32)).astype(jnp.bfloat16)
    pool = pool_ref[...]
    out_ref[...] = jnp.dot(high, pool, preferred_element_type=jnp.float32) + jnp.dot(
        low, pool, preferred_element_type=jnp.float32
    )


def pixel_sums(images):
    tiles, height, width = images.shape
    groups = LANES * EPX // width
    tiles_step = 4
    rows = tiles_step * 9 * SUBS
    pool = jnp.asarray(column_pool(width), jnp.bfloat16)
    return pl.pallas_call(
        functools.partial(pixel_kernel, tiles_step=tiles_step, groups=groups),
        grid=(tiles // tiles_step,),
        in_specs=[
            pl.BlockSpec((tiles_step, height, width), lambda i: (i, 0, 0)),
            pl.BlockSpec(pool.shape, lambda i: (0, 0)),
        ],
        out_specs=pl.BlockSpec((rows, 3 * LANES), lambda i: (i, 0)),
        out_shape=jax.ShapeDtypeStruct((tiles * 9 * SUBS, 3 * LANES), jnp.float32),
        scratch_shapes=[
            pltpu.VMEM((height + 2 * SUBS, width), jnp.float32),
            pltpu.VMEM((rows, groups * width), jnp.float32),
        ],
        compiler_params=pltpu.CompilerParams(vmem_limit_bytes=VMEM_LIMIT),
        cost_estimate=pl.CostEstimate(
            flops=tiles * 2 * 72 * 512 * 384 * 4, bytes_accessed=4 * images.size, transcendentals=0
        ),
        name="pixel_sums",
    )(images, pool)


def table_kernel(calibration_ref, direction_ref, out_ref):
    blocks = direction_ref.shape[1]
    cameras = calibration_ref.shape[0] // 6
    parts = [direction_ref[axis] for axis in range(3)]
    for camera in range(cameras):
        for motion in range(2):
            base = camera * 6 + motion * 3
            seen = calibration_ref[base] * parts[0]
            seen = seen + calibration_ref[base + 1] * parts[1]
            seen = seen + calibration_ref[base + 2] * parts[2]
            out_ref[pl.ds((motion * cameras + camera) * blocks, blocks), :] = seen


def seen_table(calibration, direction):
    _, blocks, width = direction.shape
    cameras = calibration.shape[0] // 6
    return pl.pallas_call(
        table_kernel,
        in_specs=[pl.BlockSpec(memory_space=pltpu.SMEM), pl.BlockSpec(memory_space=pltpu.VMEM)],
        out_specs=pl.BlockSpec(memory_space=pltpu.VMEM),
        out_shape=jax.ShapeDtypeStruct((2 * cameras * blocks, width), jnp.float32),
        compiler_params=pltpu.CompilerParams(vmem_limit_bytes=VMEM_LIMIT),
        cost_estimate=pl.CostEstimate(flops=10**6, bytes_accessed=2 * direction.size, transcendentals=0),
        name="seen_table",
    )(calibration, direction)


def serve_kernel(codes_ref, table_ref, out_ref):
    devices, capacity = codes_ref.shape
    half = table_ref.shape[0] // 2

    def one_device(device, carry):
        base = pl.multiple_of(device * (2 * capacity), 2 * capacity)
        for slot in range(capacity):
            code = jnp.maximum(codes_ref[device, slot], 0)
            for motion in range(2):
                out_ref[pl.ds(base + motion * capacity + slot, 1), :] = table_ref[
                    pl.ds(motion * half + code, 1), :
                ]
        return carry

    lax.fori_loop(0, devices, one_device, 0, unroll=4)


def serve(codes, table):
    devices, capacity = codes.shape
    return pl.pallas_call(
        serve_kernel,
        in_specs=[pl.BlockSpec(memory_space=pltpu.SMEM), pl.BlockSpec(memory_space=pltpu.VMEM)],
        out_specs=pl.BlockSpec(memory_space=pltpu.VMEM),
        out_shape=jax.ShapeDtypeStruct((devices * 2 * capacity, table.shape[1]), jnp.float32),
        compiler_params=pltpu.CompilerParams(vmem_limit_bytes=VMEM_LIMIT),
        name="serve",
    )(codes, table)


def request_kernel(owners_ref, local_ref, camera_ref, out_ref, *, blocks):
    owners = owners_ref[...].T
    local = local_ref[...].T
    everyone = lax.broadcasted_iota(jnp.int32, out_ref.shape, 0)
    code = camera_ref[...] * blocks
    wanted = jnp.full(out_ref.shape, -1, jnp.int32)
    for entry in range(owners.shape[0]):
        here = jnp.broadcast_to(owners[entry : entry + 1], out_ref.shape) == everyone
        wanted = jnp.where(here, jnp.broadcast_to(code + local[entry : entry + 1], out_ref.shape), wanted)
    out_ref[...] = wanted


def requests(owners, local_block, camera, blocks, devices):
    vmem = pl.BlockSpec(memory_space=pltpu.VMEM)
    return pl.pallas_call(
        functools.partial(request_kernel, blocks=blocks),
        in_specs=[vmem, vmem, vmem],
        out_specs=vmem,
        out_shape=jax.ShapeDtypeStruct((devices, owners.shape[0]), jnp.int32),
        name="requests",
    )(owners, local_block, camera.reshape(1, -1))


def tile_kernel(place_ref, arrived_ref, sums_ref, connect_ref, out_ref, parts, result, *, capacity, listed, group):
    tiles = connect_ref.shape[0]
    shape = (SUBS, LANES)
    out_ref[...] = jnp.zeros_like(out_ref)

    def one_tile(tile, parts, result):
        links = [connect_ref[tile, corner] for corner in range(4)]
        node_of = [jnp.bitwise_and(link, LANES - 1) for link in links]
        block_of = [jnp.right_shift(link, 7) for link in links]
        motion = [[jnp.zeros(shape, jnp.float32) for _ in range(2)] for _ in range(4)]
        for entry in range(listed):
            place = place_ref[tile, entry]
            rows = [
                jnp.broadcast_to(arrived_ref[pl.ds(place + axis * capacity, 1), :], shape) for axis in range(2)
            ]
            for corner in range(4):
                here = block_of[corner] == entry
                for axis in range(2):
                    picked = jnp.take_along_axis(rows[axis], node_of[corner], axis=1, mode="promise_in_bounds")
                    motion[corner][axis] = jnp.where(here, picked, motion[corner][axis])

        def element(kind, pair_y, pair_x):
            row = pl.multiple_of(tile * (9 * SUBS), SUBS) + (kind * 3 + pair_y) * SUBS
            return sums_ref[pl.ds(row, SUBS), pl.ds(pair_x * LANES, LANES)]

        for corner in range(4):
            for axis in range(2):
                total = None
                for other in range(4):
                    pair_x = corner % 2 + other % 2
                    pair_y = corner // 2 + other // 2
                    for source in range(2):
                        term = element(axis + source, pair_y, pair_x) * motion[other][source]
                        total = term if total is None else total + term
                high = total.astype(jnp.bfloat16).astype(jnp.float32)
                row = (corner * 4 + axis * 2) * SUBS
                parts[pl.ds(row, SUBS), :] = high
                parts[pl.ds(row + SUBS, SUBS), :] = total - high

        node_ids = lax.broadcasted_iota(jnp.int32, (LANES, LANES), 0)
        block_ids = lax.broadcasted_iota(jnp.int32, (listed, LANES), 0)
        total = None
        for corner in range(4):
            hots = []
            spreads = []
            for chunk in range(SUBS):
                link = connect_ref[tile, corner, pl.ds(chunk, 1), :]
                nodes = jnp.broadcast_to(jnp.bitwise_and(link, LANES - 1), (LANES, LANES))
                hots.append(jnp.where(nodes == node_ids, 1.0, 0.0).astype(jnp.bfloat16))
                here = jnp.broadcast_to(jnp.right_shift(link, 7), (listed, LANES)) == block_ids
                chosen = []
                for part in range(4):
                    row = parts[pl.ds((corner * 4 + part) * SUBS + chunk, 1), :]
                    chosen.append(jnp.where(here, jnp.broadcast_to(row, (listed, LANES)), 0.0).astype(jnp.bfloat16))
                spreads.append(jnp.concatenate(chosen, axis=0))
            term = lax.dot_general(
                jnp.concatenate(spreads, axis=1),
                jnp.concatenate(hots, axis=1),
                (((1,), (1,)), ((), ())),
                preferred_element_type=jnp.float32,
            )
            total = term if total is None else total + term
        for axis in range(2):
            base = 2 * axis * listed
            result[pl.ds(axis * listed, listed), :] = (
                total[base : base + listed] + total[base + listed : base + 2 * listed]
            )
        for entry in range(listed):
            place = place_ref[tile, entry]
            for axis in range(2):
                out_ref[pl.ds(place + axis * capacity, 1), :] = result[pl.ds(axis * listed + entry, 1), :]

    def one_group(step, carry):
        for member in range(group):
            one_tile(step * group + member, parts.at[member], result.at[member])
        return carry

    lax.fori_loop(0, tiles // group, one_group, 0)


def tile_forces(places, arrived, sums, connect, capacity):
    tiles, listed = places.shape
    group = math.gcd(tiles, 8)
    vmem = pl.BlockSpec(memory_space=pltpu.VMEM)
    return pl.pallas_call(
        functools.partial(tile_kernel, capacity=capacity, listed=listed, group=group),
        in_specs=[pl.BlockSpec(memory_space=pltpu.SMEM), vmem, vmem, vmem],
        out_specs=vmem,
        out_shape=jax.ShapeDtypeStruct(arrived.shape, jnp.float32),
        scratch_shapes=[
            pltpu.VMEM((group, 16 * SUBS, LANES), jnp.float32),
            pltpu.VMEM((group, 2 * listed, LANES), jnp.float32),
        ],
        compiler_params=pltpu.CompilerParams(vmem_limit_bytes=VMEM_LIMIT),
        name="tile_forces",
    )(places, arrived, sums, connect)


def hot_kernel(codes_ref, direction_ref, damping_ref, hot_ref, damped_ref):
    for part in range(codes_ref.shape[0]):
        ids = lax.broadcasted_iota(jnp.int32, (hot_ref.shape[0], LANES), 0)
        here = jnp.broadcast_to(codes_ref[pl.ds(part, 1), :], ids.shape) == ids
        hot_ref[:, pl.ds(part * LANES, LANES)] = jnp.where(here, 1.0, 0.0).astype(jnp.bfloat16)
    damped_ref[...] = damping_ref[...] * direction_ref[...]


def hot_table(codes, direction, damping, cameras):
    vmem = pl.BlockSpec(memory_space=pltpu.VMEM)
    shape = (cameras * direction.shape[1], codes.size)
    return pl.pallas_call(
        hot_kernel,
        in_specs=[vmem, vmem, vmem],
        out_specs=(vmem, vmem),
        out_shape=(
            jax.ShapeDtypeStruct(shape, jnp.bfloat16),
            jax.ShapeDtypeStruct(direction.shape, jnp.float32),
        ),
        compiler_params=pltpu.CompilerParams(vmem_limit_bytes=VMEM_LIMIT),
        cost_estimate=pl.CostEstimate(flops=10**6, bytes_accessed=10**6, transcendentals=0),
        name="hot_table",
    )(codes, direction, damping)


def finish_kernel(calibration_ref, hot_ref, back_ref, damped_ref, out_ref, *, capacity, devices):
    blocks = damped_ref.shape[1]
    cameras = calibration_ref.shape[0] // 6
    slots = devices * capacity
    back = back_ref[...].reshape(devices, 2, capacity, LANES)
    halves = []
    for motion in range(2):
        values = back[:, motion].reshape(slots, LANES)
        high = values.astype(jnp.bfloat16)
        halves += [high, (values - high.astype(jnp.float32)).astype(jnp.bfloat16)]
    right = jnp.concatenate(halves, axis=1)
    totals = [damped_ref[axis] for axis in range(3)]
    for camera in range(cameras):
        summed = jnp.dot(
            hot_ref[pl.ds(camera * blocks, blocks), :], right, preferred_element_type=jnp.float32
        )
        for motion in range(2):
            base = 2 * motion * LANES
            seen = summed[:, base : base + LANES] + summed[:, base + LANES : base + 2 * LANES]
            for axis in range(3):
                totals[axis] = totals[axis] + calibration_ref[camera * 6 + motion * 3 + axis] * seen
    for axis in range(3):
        out_ref[axis] = totals[axis]


def finish(calibration, hot, back, damped, capacity, devices):
    vmem = pl.BlockSpec(memory_space=pltpu.VMEM)
    return pl.pallas_call(
        functools.partial(finish_kernel, capacity=capacity, devices=devices),
        in_specs=[pl.BlockSpec(memory_space=pltpu.SMEM), vmem, vmem, vmem],
        out_specs=vmem,
        out_shape=jax.ShapeDtypeStruct(damped.shape, jnp.float32),
        compiler_params=pltpu.CompilerParams(vmem_limit_bytes=VMEM_LIMIT),
        name="finish",
    )(calibration, hot, back, damped)


def exchange(values):
    return lax.all_to_all(values, AXES, split_axis=0, concat_axis=0, tiled=True)


def per_device(images, direction, damping, calibration, camera, owners, local_block, connect):
    devices = lax.axis_size(AXES)
    tiles, listed = owners.shape
    blocks, _, width = direction.shape
    cameras = calibration.shape[0]
    capacity = max(2, min(tiles, 4 * tiles * listed // devices))
    direction = direction.transpose(1, 0, 2)
    damping = damping.transpose(1, 0, 2)
    calibration = calibration.reshape(-1)
    if capacity == tiles:
        wanted = requests(owners, local_block, camera, blocks, devices)
        slot = jnp.broadcast_to(jnp.arange(tiles, dtype=jnp.int32)[:, None], owners.shape)
    else:
        everyone = jnp.arange(devices, dtype=jnp.int32)
        code = camera[:, None] * blocks + local_block
        hits = owners[None, :, :] == everyone[:, None, None]
        named = jnp.sum(jnp.where(hits, code[None] + 1, 0), axis=2)
        taken = (named > 0).astype(jnp.int32)
        rank = jnp.cumsum(taken, axis=1) - taken
        slots = jnp.arange(capacity, dtype=jnp.int32)
        chosen = (rank[:, :, None] == slots[None, None, :]) & (taken[:, :, None] > 0)
        wanted = jnp.sum(jnp.where(chosen, named[:, :, None], 0), axis=1) - 1
        slot = jnp.sum(jnp.where(hits, rank[:, :, None], 0), axis=0)
    places = owners * (2 * capacity) + slot
    asked = exchange(wanted.reshape(devices, 1, capacity)).reshape(devices, capacity)
    table = seen_table(calibration, direction)
    sums = pixel_sums(images)
    outgoing = serve(asked, table)
    shape = (devices, 2 * capacity, width)
    arrived = exchange(outgoing.reshape(shape)).reshape(-1, width)
    hot, damped = hot_table(asked.reshape(-1, LANES), direction, damping, cameras)
    forces = tile_forces(places, arrived, sums, connect.reshape(tiles, 4, SUBS, LANES), capacity)
    back = exchange(forces.reshape(shape)).reshape(-1, width)
    product = finish(calibration, hot, back, damped, capacity, devices)
    return product.transpose(1, 0, 2)


def solution(mesh):
    split = P(AXES)
    return jax.shard_map(
        per_device,
        mesh=mesh,
        in_specs=(split, split, split, P(), split, split, split, split),
        out_specs=split,
        check_vma=False,
    )
```

time: 73.3 us -> 64.7 us (0.88)
  Pallas kernels: 21 us -> 17.2 us
  other arithmetic: 2.98 us -> 0.69 us
  waiting for transfers between devices: 32.2 us -> 30.5 us
  local copies, waits for them, and re-layouts: 3.35 us -> 2.52 us
    pallas_call x1, Pallas kernels: 14.2 us -> 8.3 us  [tile_forces(): pl.pallas_call(functools.partial(tile_kernel, capacity=capacity, listed=l...]
    pallas_call x1 -> x4, Pallas kernels: 2.33 us -> 4.5 us  [the longest x1 2.31 us: serve(): pl.pallas_call(serve_kernel, in_specs=[pl.BlockSpec(memory_space=pltpu.SM...]
    all_to_all x3, waiting for transfers between devices: 32.2 us -> 30.5 us  [exchange(): return lax.all_to_all(values, AXES, split_axis=0, concat_axis=0, tiled=True)]
    reduce_sum x1 -> x0, other arithmetic: 0.84 us -> none  [per_device(): named = jnp.sum(jnp.where(hits, code[None] + 1, 0), axis=2)]
    add x2 -> x1, other arithmetic: 0.77 us -> 0.01 us  [per_device(): places = owners * (2 * capacity) + slot]
  transfers between devices with their start and end apart: 3 -> 3, of which waited for: 3 -> 3; matrix products, arithmetic and copies ran while one was open for 3% -> 4% of each run, Pallas kernels for 4% -> 6%
where the time goes in v2:
time: 64.7 us; the launch traced here: 64.2 us
  waiting for transfers between devices  30.5 us (47%)
  Pallas kernels  17.2 us (27%)
  starting transfers between devices  13.2 us (20%)
  local copies, waits for them, and re-layouts  2.52 us (4%)
  other arithmetic  0.69 us (1%)
    all_to_all x3, waiting for transfers between devices, exchange(): return lax.all_to_all(values, AXES, split_axis=0, concat_axis=0, tiled=True)  30.5 us
    all_to_all x3, starting transfers between devices, exchange(): return lax.all_to_all(values, AXES, split_axis=0, concat_axis=0, tiled=True)  13.2 us
    pallas_call x1, Pallas kernels, tile_forces(): pl.pallas_call(functools.partial(tile_kernel, capacity=capacity, listed=l...  8.3 us
    pallas_call x1, Pallas kernels, pixel_sums(): pl.pallas_call(functools.partial(pixel_kernel, tiles_step=tiles_step, gro...  2.78 us
    pallas_call x1, Pallas kernels, serve(): pl.pallas_call(serve_kernel, in_specs=[pl.BlockSpec(memory_space=pltpu.SM...  2.31 us
    unnamed x15, local copies, waits for them, and re-layouts  1.73 us
    pallas_call x1, Pallas kernels, finish(): pl.pallas_call(functools.partial(finish_kernel, capacity=capacity, device...  1.67 us
    pallas_call x1, Pallas kernels, requests(): pl.pallas_call(functools.partial(request_kernel, blocks=blocks), in_specs...  1.42 us
  transfers between devices with their start and end apart: 3, of which 3 were waited for; matrix products, arithmetic and copies ran while one was open for 4% of the time, Pallas kernels for 6%

profile of v2, /device:TPU:1, one launch (start us, length us, event | category | flops | bytes accessed | tf_op | source)
XLA Modules:
  0.0 64.2 jit_solution(6400453717357439764)
XLA Ops:
  0.0 1.4 %requests.1 = s32[32,16]{1,0:T(8,128)} custom-call(s32[16,16]{1,0:T(8,128)} %owners_ref.1, s32[16,16]{1,0:T(8,128)} %local_ref.1, s32[1,16]{1,0:T(1,128)} %bitcast.19), custom_call_target="tpu_custom_call" | custom-call | tf_op jit(solution)/shard_map/requests/pallas_call | solution.py:177
  1.4 7.1 %all-to-all-start = ((s32[32,1,16]{2,1,0:T(1,128)}), s32[32,1,16]{2,1,0:T(1,128)S(1)}, u32[]{:S(2)}, u32[]{:S(2)}) async-start(s32[32,1,16]{2,1,0:T(1,128)} %bitcast.18), calls=%async_computation | async-start | bytes 32768 | tf_op jit(solution)/shard_map/all_to_all | solution.py:347
  8.5 0.8 %copy.12 = f32[4,2,3]{2,1,0:T(2,128)S(1)} copy(f32[4,2,3]{0,1,2:T(2,128)} %param.12) | data formatting | bytes 192 | tf_op args[3]
  9.3 0.1 reshape.27.calibration_ref
  9.4 0.9 %copy-done = f32[128,3,128]{2,0,1:T(8,128)S(1)} copy-done((f32[128,3,128]{2,0,1:T(8,128)S(1)}, f32[128,3,128]{2,0,1:T(8,128)}, u32[]{:S(2)}) %copy-start) | copy-done | bytes 196632
  10.3 0.6 seen_table.1.table_ref
  11.0 4.2 %all-to-all-done = s32[32,1,16]{2,1,0:T(1,128)S(1)} async-done(((s32[32,1,16]{2,1,0:T(1,128)}), s32[32,1,16]{2,1,0:T(1,128)S(1)}, u32[]{:S(2)}, u32[]{:S(2)}) %all-to-all-start) | async-done | bytes 2080 | tf_op jit(solution)/shard_map/all_to_all | solution.py:347
  15.1 2.3 %serve.1 = f32[1024,128]{1,0:T(8,128)} custom-call(s32[32,16]{1,0:T(8,128)S(1)} %bitcast.17, f32[1024,128]{1,0:T(8,128)S(1)} %seen_table.1.table_ref), custom_call_target="tpu_custom_call" | custom-call | tf_op jit(solution)/shard_map/serve/pallas_call | solution.py:153
  17.4 2.9 %all-to-all-start.1 = ((f32[32,32,128]{2,1,0:T(8,128)}), f32[32,32,128]{2,1,0:T(8,128)S(1)}, u32[]{:S(2)}, u32[]{:S(2)}) async-start(f32[32,32,128]{2,1,0:T(8,128)} %bitcast.6), calls=%async_computation.1 | async-start | bytes 1048576 | tf_op jit(solution)/shard_map/all_to_all | solution.py:347
  20.4 0.0 copy-done.5
  20.4 0.1 reshape.33.connect_ref
  20.5 0.0 copy-start.6
  20.6 2.8 %pixel_sums.1.sums_ref = f32[1152,384]{1,0:T(8,128)S(1)} custom-call(bf16[16,128,128]{2,1,0:T(8,128)(2,1)S(1)} %copy-done.3, bf16[512,384]{1,0:T(8,128)(2,1)S(1)} %copy-done.4), custom_call_target="tpu_custom_call" | custom-call | flops 1811939328 | bytes 1048576 | tf_op jit(solution)/shard_map/pixel_sums/pallas_call | solution.py:86
  23.3 0.0 copy-done.6
  23.4 12.5 %all-to-all-done.1 = f32[32,32,128]{2,1,0:T(8,128)S(1)} async-done(((f32[32,32,128]{2,1,0:T(8,128)}), f32[32,32,128]{2,1,0:T(8,128)S(1)}, u32[]{:S(2)}, u32[]{:S(2)}) %all-to-all-start.1) | async-done | bytes 524320 | tf_op jit(solution)/shard_map/all_to_all | solution.py:347
  35.8 8.3 %tile_forces.1 = f32[1024,128]{1,0:T(8,128)} custom-call(s32[16,16]{1,0:T(8,128)S(1)} %iota_add_fusion.place_ref, f32[1024,128]{1,0:T(8,128)S(1)} %bitcast.13, f32[1152,384]{1,0:T(8,128)S(1)} %pixel_sums.1.sums_ref, s32[16,4,8,128]{3,2,1,0:T(8,128)S(1)} %reshape.33.connect_ref), custom_call_target="tpu_custom_call" | custom-call | tf_op jit(solution)/shard_map/tile_forces/pallas_call | solution.py:270
  44.1 3.1 %all-to-all-start.2 = ((f32[32,32,128]{2,1,0:T(8,128)}), f32[32,32,128]{2,1,0:T(8,128)S(1)}, u32[]{:S(2)}, u32[]{:S(2)}) async-start(f32[32,32,128]{2,1,0:T(8,128)} %bitcast.8), calls=%async_computation.2 | async-start | bytes 1048576 | tf_op jit(solution)/shard_map/all_to_all | solution.py:347
  47.3 0.5 broadcast.3
  47.8 0.7 %reduce.3 = s32[32,16]{1,0:T(8,128)S(1)} reduce(s32[32,1,16]{2,1,0:T(1,128)S(1)} %all-to-all-done, s32[]{:T(128)} %broadcast.3), dimensions={1}, to_apply=%all_to_all.9.reduce_sub_computation.3 | reduce | bytes 4100 | tf_op jit(solution)/shard_map/all_to_all | solution.py:347
  48.5 0.1 reshape_reshape.3.codes_ref
  48.5 0.0 copy-done.2
  48.5 0.1 hot_table.1
  48.7 13.9 %all-to-all-done.2 = f32[32,32,128]{2,1,0:T(8,128)S(1)} async-done(((f32[32,32,128]{2,1,0:T(8,128)}), f32[32,32,128]{2,1,0:T(8,128)S(1)}, u32[]{:S(2)}, u32[]{:S(2)}) %all-to-all-start.2) | async-done | bytes 524320 | tf_op jit(solution)/shard_map/all_to_all | solution.py:347
  62.6 1.7 %finish.1 = f32[3,128,128]{2,1,0:T(8,128)} custom-call(f32[24]{0:T(128)S(1)} %reshape.27.calibration_ref, bf16[512,512]{1,0:T(8,128)(2,1)S(1)} %get-tuple-element.7.hot_ref, f32[1024,128]{1,0:T(8,128)S(1)} %bitcast.12, f32[3,128,128]{2,1,0:T(8,128)S(1)} %get-tuple-element.8.damped_ref), custom_call_target="tpu_custom_call" | custom-call | tf_op jit(solution)/shard_map/finish/pallas_call | solution.py:336
  (10 shorter events, 0.0 us)
Async XLA Ops:
  1.4 13.7 %all-to-all-start = ((s32[32,1,16]{2,1,0:T(1,128)}), s32[32,1,16]{2,1,0:T(1,128)S(1)}, u32[]{:S(2)}, u32[]{:S(2)}) async-start(s32[32,1,16]{2,1,0:T(1,128)} %bitcast.18), calls=%async_computation | async-start | bytes 32768 | tf_op jit(solution)/shard_map/all_to_all | solution.py:347
  9.4 0.9 %copy-start = (f32[128,3,128]{2,0,1:T(8,128)S(1)}, f32[128,3,128]{2,0,1:T(8,128)}, u32[]{:S(2)}) copy-start(f32[128,3,128]{2,0,1:T(8,128)} %param.10) | copy-start | bytes 589828
  10.3 10.1 %copy-start.5 = (s32[16,4,1024]{2,1,0:T(4,128)S(1)}, s32[16,4,1024]{2,1,0:T(4,128)}, u32[]{:S(2)}) copy-start(s32[16,4,1024]{2,1,0:T(4,128)} %param.16) | copy-start | bytes 786436
  10.3 10.2 %copy-start.3 = (bf16[16,128,128]{2,1,0:T(8,128)(2,1)S(1)}, bf16[16,128,128]{2,1,0:T(8,128)(2,1)}, u32[]{:S(2)}) copy-start(bf16[16,128,128]{2,1,0:T(8,128)(2,1)} %images_ref.1) | copy-start | bytes 1572868
  10.3 10.2 %copy-start.4 = (bf16[512,384]{1,0:T(8,128)(2,1)S(1)}, bf16[512,384]{1,0:T(8,128)(2,1)}, u32[]{:S(2)}) copy-start(bf16[512,384]{1,0:T(8,128)(2,1)} %constant.4.clone.pool_ref) | copy-start | bytes 1179652
  17.4 18.4 %all-to-all-start.1 = ((f32[32,32,128]{2,1,0:T(8,128)}), f32[32,32,128]{2,1,0:T(8,128)S(1)}, u32[]{:S(2)}, u32[]{:S(2)}) async-start(f32[32,32,128]{2,1,0:T(8,128)} %bitcast.6), calls=%async_computation.1 | async-start | bytes 1048576 | tf_op jit(solution)/shard_map/all_to_all | solution.py:347
  20.5 2.8 %copy-start.6 = (s32[16,16]{1,0:T(8,128)S(1)}, s32[16,16]{1,0:T(8,128)}, u32[]{:S(2)}) copy-start(s32[16,16]{1,0:T(8,128)} %owners_ref.1) | copy-start | bytes 3076
  35.8 12.7 %copy-start.1 = (f32[128,3,128]{2,0,1:T(8,128)S(1)}, f32[128,3,128]{2,0,1:T(8,128)}, u32[]{:S(2)}) copy-start(f32[128,3,128]{2,0,1:T(8,128)} %param.10) | copy-start | bytes 589828
  35.8 12.7 %copy-start.2 = (f32[128,3,128]{2,0,1:T(8,128)S(1)}, f32[128,3,128]{2,0,1:T(8,128)}, u32[]{:S(2)}) copy-start(f32[128,3,128]{2,0,1:T(8,128)} %param.11) | copy-start | bytes 589828
  44.1 18.4 %all-to-all-start.2 = ((f32[32,32,128]{2,1,0:T(8,128)}), f32[32,32,128]{2,1,0:T(8,128)S(1)}, u32[]{:S(2)}, u32[]{:S(2)}) async-start(f32[32,32,128]{2,1,0:T(8,128)} %bitcast.8), calls=%async_computation.2 | async-start | bytes 1048576 | tf_op jit(solution)/shard_map/all_to_all | solution.py:347

commit v3 on v2

--- a/solution.py
+++ b/solution.py
@@ -107,6 +107,7 @@
 def table_kernel(calibration_ref, direction_ref, out_ref):
     blocks = direction_ref.shape[1]
     cameras = calibration_ref.shape[0] // 6
+    half = cameras * blocks
     parts = [direction_ref[axis] for axis in range(3)]
     for camera in range(cameras):
         for motion in range(2):
@@ -114,7 +115,8 @@
             seen = calibration_ref[base] * parts[0]
             seen = seen + calibration_ref[base + 1] * parts[1]
             seen = seen + calibration_ref[base + 2] * parts[2]
-            out_ref[pl.ds((motion * cameras + camera) * blocks, blocks), :] = seen
+            out_ref[pl.ds(motion * half + camera * blocks, blocks), :] = seen
+    out_ref[pl.ds(2 * half, 2 * SUBS), :] = jnp.zeros((2 * SUBS, out_ref.shape[1]), jnp.float32)
 
 
 def seen_table(calibration, direction):
@@ -124,58 +126,63 @@
         table_kernel,
         in_specs=[pl.BlockSpec(memory_space=pltpu.SMEM), pl.BlockSpec(memory_space=pltpu.VMEM)],
         out_specs=pl.BlockSpec(memory_space=pltpu.VMEM),
-        out_shape=jax.ShapeDtypeStruct((2 * cameras * blocks, width), jnp.float32),
+        out_shape=jax.ShapeDtypeStruct((2 * (cameras * blocks + SUBS), width), jnp.float32),
         compiler_params=pltpu.CompilerParams(vmem_limit_bytes=VMEM_LIMIT),
         cost_estimate=pl.CostEstimate(flops=10**6, bytes_accessed=2 * direction.size, transcendentals=0),
         name="seen_table",
     )(calibration, direction)
 
 
-def serve_kernel(codes_ref, table_ref, out_ref):
-    devices, capacity = codes_ref.shape
-    half = table_ref.shape[0] // 2
-
-    def one_device(device, carry):
-        base = pl.multiple_of(device * (2 * capacity), 2 * capacity)
-        for slot in range(capacity):
-            code = jnp.maximum(codes_ref[device, slot], 0)
-            for motion in range(2):
-                out_ref[pl.ds(base + motion * capacity + slot, 1), :] = table_ref[
-                    pl.ds(motion * half + code, 1), :
-                ]
-        return carry
-
-    lax.fori_loop(0, devices, one_device, 0, unroll=4)
+def serve_kernel(codes_ref, table_ref, out_ref, rows, sems, *, capacity):
+    devices = codes_ref.shape[0] // capacity
+    half = table_ref.shape[0] // 2 - SUBS
+    pieces = sems.shape[0]
+    length = rows.shape[0] // pieces
+    copies = []
+    for piece in range(pieces):
+        for device in range(piece * devices // pieces, (piece + 1) * devices // pieces):
+            for slot in range(capacity):
+                code = codes_ref[device * capacity + slot]
+                for motion in range(2):
+                    row = device * (2 * capacity) + motion * capacity + slot
+                    rows[pl.ds(row, 1), :] = table_ref[pl.ds(motion * half + code, 1), :]
+        place = pl.ds(piece * length, length)
+        copies.append(pltpu.make_async_copy(rows.at[place], out_ref.at[place], sems.at[piece]))
+        copies[-1].start()
+    for copy in copies:
+        copy.wait()
 
 
 def serve(codes, table):
     devices, capacity = codes.shape
-    return pl.pallas_call(
-        serve_kernel,
+    shape = (devices * 2 * capacity, table.shape[1])
+    return pl.pallas_call(
+        functools.partial(serve_kernel, capacity=capacity),
         in_specs=[pl.BlockSpec(memory_space=pltpu.SMEM), pl.BlockSpec(memory_space=pltpu.VMEM)],
-        out_specs=pl.BlockSpec(memory_space=pltpu.VMEM),
-        out_shape=jax.ShapeDtypeStruct((devices * 2 * capacity, table.shape[1]), jnp.float32),
+        out_specs=pl.BlockSpec(memory_space=pl.ANY),
+        out_shape=jax.ShapeDtypeStruct(shape, jnp.float32),
+        scratch_shapes=[pltpu.VMEM(shape, jnp.float32), pltpu.SemaphoreType.DMA((math.gcd(devices, 8),))],
         compiler_params=pltpu.CompilerParams(vmem_limit_bytes=VMEM_LIMIT),
         name="serve",
-    )(codes, table)
-
-
-def request_kernel(owners_ref, local_ref, camera_ref, out_ref, *, blocks):
+    )(codes.reshape(-1), table)
+
+
+def request_kernel(owners_ref, local_ref, camera_ref, out_ref, *, blocks, nothing):
     owners = owners_ref[...].T
     local = local_ref[...].T
     everyone = lax.broadcasted_iota(jnp.int32, out_ref.shape, 0)
     code = camera_ref[...] * blocks
-    wanted = jnp.full(out_ref.shape, -1, jnp.int32)
+    wanted = jnp.full(out_ref.shape, nothing, jnp.int32)
     for entry in range(owners.shape[0]):
         here = jnp.broadcast_to(owners[entry : entry + 1], out_ref.shape) == everyone
         wanted = jnp.where(here, jnp.broadcast_to(code + local[entry : entry + 1], out_ref.shape), wanted)
     out_ref[...] = wanted
 
 
-def requests(owners, local_block, camera, blocks, devices):
+def requests(owners, local_block, camera, blocks, devices, nothing):
     vmem = pl.BlockSpec(memory_space=pltpu.VMEM)
     return pl.pallas_call(
-        functools.partial(request_kernel, blocks=blocks),
+        functools.partial(request_kernel, blocks=blocks, nothing=nothing),
         in_specs=[vmem, vmem, vmem],
         out_specs=vmem,
         out_shape=jax.ShapeDtypeStruct((devices, owners.shape[0]), jnp.int32),
@@ -193,16 +200,15 @@
         node_of = [jnp.bitwise_and(link, LANES - 1) for link in links]
         block_of = [jnp.right_shift(link, 7) for link in links]
         motion = [[jnp.zeros(shape, jnp.float32) for _ in range(2)] for _ in range(4)]
-        for entry in range(listed):
-            place = place_ref[tile, entry]
-            rows = [
-                jnp.broadcast_to(arrived_ref[pl.ds(place + axis * capacity, 1), :], shape) for axis in range(2)
-            ]
-            for corner in range(4):
-                here = block_of[corner] == entry
-                for axis in range(2):
-                    picked = jnp.take_along_axis(rows[axis], node_of[corner], axis=1, mode="promise_in_bounds")
-                    motion[corner][axis] = jnp.where(here, picked, motion[corner][axis])
+        places = [place_ref[tile * listed + entry] for entry in range(listed)]
+        for corner in range(4):
+            for axis in range(2):
+                for entry in range(listed):
+                    row = arrived_ref[pl.ds(places[entry] + axis * capacity, 1), :]
+                    picked = jnp.take_along_axis(
+                        jnp.broadcast_to(row, shape), node_of[corner], axis=1, mode="promise_in_bounds"
+                    )
+                    motion[corner][axis] = jnp.where(block_of[corner] == entry, picked, motion[corner][axis])
 
         def element(kind, pair_y, pair_x):
             row = pl.multiple_of(tile * (9 * SUBS), SUBS) + (kind * 3 + pair_y) * SUBS
@@ -251,9 +257,8 @@
                 total[base : base + listed] + total[base + listed : base + 2 * listed]
             )
         for entry in range(listed):
-            place = place_ref[tile, entry]
             for axis in range(2):
-                out_ref[pl.ds(place + axis * capacity, 1), :] = result[pl.ds(axis * listed + entry, 1), :]
+                out_ref[pl.ds(places[entry] + axis * capacity, 1), :] = result[pl.ds(axis * listed + entry, 1), :]
 
     def one_group(step, carry):
         for member in range(group):
@@ -265,7 +270,7 @@
 
 def tile_forces(places, arrived, sums, connect, capacity):
     tiles, listed = places.shape
-    group = math.gcd(tiles, 8)
+    group = math.gcd(tiles, 16)
     vmem = pl.BlockSpec(memory_space=pltpu.VMEM)
     return pl.pallas_call(
         functools.partial(tile_kernel, capacity=capacity, listed=listed, group=group),
@@ -278,7 +283,7 @@
         ],
         compiler_params=pltpu.CompilerParams(vmem_limit_bytes=VMEM_LIMIT),
         name="tile_forces",
-    )(places, arrived, sums, connect)
+    )(places.reshape(-1), arrived, sums, connect)
 
 
 def hot_kernel(codes_ref, direction_ref, damping_ref, hot_ref, damped_ref):
@@ -306,7 +311,7 @@
     )(codes, direction, damping)
 
 
-def finish_kernel(calibration_ref, hot_ref, back_ref, damped_ref, out_ref, *, capacity, devices):
+def finish_kernel(calibration_ref, hot_ref, back_ref, damped_ref, out_ref, rows, sems, *, capacity, devices):
     blocks = damped_ref.shape[1]
     cameras = calibration_ref.shape[0] // 6
     slots = devices * capacity
@@ -317,30 +322,37 @@
         high = values.astype(jnp.bfloat16)
         halves += [high, (values - high.astype(jnp.float32)).astype(jnp.bfloat16)]
     right = jnp.concatenate(halves, axis=1)
-    totals = [damped_ref[axis] for axis in range(3)]
-    for camera in range(cameras):
-        summed = jnp.dot(
-            hot_ref[pl.ds(camera * blocks, blocks), :], right, preferred_element_type=jnp.float32
-        )
-        for motion in range(2):
-            base = 2 * motion * LANES
-            seen = summed[:, base : base + LANES] + summed[:, base + LANES : base + 2 * LANES]
-            for axis in range(3):
-                totals[axis] = totals[axis] + calibration_ref[camera * 6 + motion * 3 + axis] * seen
+    summed = jnp.dot(hot_ref[...], right, preferred_element_type=jnp.float32)
+    seen = []
+    for motion in range(2):
+        base = 2 * motion * LANES
+        seen.append(summed[:, base : base + LANES] + summed[:, base + LANES : base + 2 * LANES])
+    copies = []
     for axis in range(3):
-        out_ref[axis] = totals[axis]
+        total = damped_ref[axis]
+        for camera in range(cameras):
+            for motion in range(2):
+                factor = calibration_ref[pl.ds(camera * 6 + motion * 3 + axis, 1), :]
+                total = total + factor * seen[motion][camera * blocks : (camera + 1) * blocks]
+        rows[axis] = total
+        copies.append(pltpu.make_async_copy(rows.at[axis], out_ref.at[axis], sems.at[axis]))
+        copies[-1].start()
+    for copy in copies:
+        copy.wait()
 
 
 def finish(calibration, hot, back, damped, capacity, devices):
     vmem = pl.BlockSpec(memory_space=pltpu.VMEM)
+    spread = jnp.broadcast_to(calibration[:, None], (calibration.shape[0], LANES))
     return pl.pallas_call(
         functools.partial(finish_kernel, capacity=capacity, devices=devices),
-        in_specs=[pl.BlockSpec(memory_space=pltpu.SMEM), vmem, vmem, vmem],
-        out_specs=vmem,
+        in_specs=[vmem, vmem, vmem, vmem],
+        out_specs=pl.BlockSpec(memory_space=pl.ANY),
         out_shape=jax.ShapeDtypeStruct(damped.shape, jnp.float32),
+        scratch_shapes=[pltpu.VMEM(damped.shape, jnp.float32), pltpu.SemaphoreType.DMA((3,))],
         compiler_params=pltpu.CompilerParams(vmem_limit_bytes=VMEM_LIMIT),
         name="finish",
-    )(calibration, hot, back, damped)
+    )(spread, hot, back, damped)
 
 
 def exchange(values):
@@ -357,7 +369,7 @@
     damping = damping.transpose(1, 0, 2)
     calibration = calibration.reshape(-1)
     if capacity == tiles:
-        wanted = requests(owners, local_block, camera, blocks, devices)
+        wanted = requests(owners, local_block, camera, blocks, devices, cameras * blocks)
         slot = jnp.broadcast_to(jnp.arange(tiles, dtype=jnp.int32)[:, None], owners.shape)
     else:
         everyone = jnp.arange(devices, dtype=jnp.int32)
@@ -368,7 +380,8 @@
         rank = jnp.cumsum(taken, axis=1) - taken
         slots = jnp.arange(capacity, dtype=jnp.int32)
         chosen = (rank[:, :, None] == slots[None, None, :]) & (taken[:, :, None] > 0)
-        wanted = jnp.sum(jnp.where(chosen, named[:, :, None], 0), axis=1) - 1
+        wanted = jnp.sum(jnp.where(chosen, named[:, :, None], 0), axis=1)
+        wanted = jnp.where(wanted > 0, wanted - 1, cameras * blocks)
         slot = jnp.sum(jnp.where(hits, rank[:, :, None], 0), axis=0)
     places = owners * (2 * capacity) + slot
     asked = exchange(wanted.reshape(devices, 1, capacity)).reshape(devices, capacity)

time: 64.7 us -> 62.8 us (0.971)
  Pallas kernels: 17.2 us -> 15.2 us
    pallas_call x1, Pallas kernels: 8.3 us -> 7.24 us  [tile_forces(): pl.pallas_call(functools.partial(tile_kernel, capacity=capacity, listed=l...]
where the time goes in v3:
time: 62.8 us; the launch traced here: 62.4 us
  waiting for transfers between devices  30.4 us (48%)
  Pallas kernels  15.2 us (24%)
  starting transfers between devices  13.2 us (21%)
  local copies, waits for them, and re-layouts  2.74 us (4%)
  other arithmetic  0.69 us (1%)
    all_to_all x3, waiting for transfers between devices, exchange(): return lax.all_to_all(values, AXES, split_axis=0, concat_axis=0, tiled=True)  30.4 us
    all_to_all x3, starting transfers between devices, exchange(): return lax.all_to_all(values, AXES, split_axis=0, concat_axis=0, tiled=True)  13.2 us
    pallas_call x1, Pallas kernels, tile_forces(): pl.pallas_call(functools.partial(tile_kernel, capacity=capacity, listed=l...  7.24 us
    pallas_call x1, Pallas kernels, pixel_sums(): pl.pallas_call(functools.partial(pixel_kernel, tiles_step=tiles_step, gro...  2.78 us
    pallas_call x1, Pallas kernels, serve(): pl.pallas_call(functools.partial(serve_kernel, capacity=capacity), in_spe...  1.8 us
    unnamed x15, local copies, waits for them, and re-layouts  1.73 us
    pallas_call x1, Pallas kernels, requests(): pl.pallas_call(functools.partial(request_kernel, blocks=blocks, nothing=n...  1.47 us
  transfers between devices with their start and end apart: 3, of which 3 were waited for; matrix products, arithmetic and copies ran while one was open for 4% of the time, Pallas kernels for 6%

profile of v3, /device:TPU:1, one launch (start us, length us, event | category | flops | bytes accessed | tf_op | source)
XLA Modules:
  0.0 62.4 jit_solution(3765981047328050642)
XLA Ops:
  0.0 1.5 %requests.1 = s32[32,16]{1,0:T(8,128)} custom-call(s32[16,16]{1,0:T(8,128)} %owners_ref.1, s32[16,16]{1,0:T(8,128)} %local_ref.1, s32[1,16]{1,0:T(1,128)} %bitcast.19), custom_call_target="tpu_custom_call" | custom-call | tf_op jit(solution)/shard_map/requests/pallas_call | solution.py:184
  1.5 7.1 %all-to-all-start = ((s32[32,1,16]{2,1,0:T(1,128)}), s32[32,1,16]{2,1,0:T(1,128)S(1)}, u32[]{:S(2)}, u32[]{:S(2)}) async-start(s32[32,1,16]{2,1,0:T(1,128)} %bitcast.18), calls=%async_computation | async-start | bytes 32768 | tf_op jit(solution)/shard_map/all_to_all | solution.py:359
  8.6 0.8 %copy.12 = f32[4,2,3]{2,1,0:T(2,128)S(1)} copy(f32[4,2,3]{0,1,2:T(2,128)} %param.12) | data formatting | bytes 192 | tf_op args[3]
  9.4 0.1 broadcast_in_dim.6.calibration_ref
  9.4 0.9 %copy-done = f32[128,3,128]{2,0,1:T(8,128)S(1)} copy-done((f32[128,3,128]{2,0,1:T(8,128)S(1)}, f32[128,3,128]{2,0,1:T(8,128)}, u32[]{:S(2)}) %copy-start) | copy-done | bytes 196632
  10.4 0.6 %seen_table.1.table_ref = f32[1040,128]{1,0:T(8,128)S(1)} custom-call(f32[24]{0:T(128)S(1)} %broadcast_in_dim.6.calibration_ref, f32[3,128,128]{2,1,0:T(8,128)S(1)} %bitcast.14), custom_call_target="tpu_custom_call" | custom-call | flops 1000000 | bytes 98304 | tf_op jit(solution)/shard_map/seen_table/pallas_call | solution.py:125
  11.0 4.2 %all-to-all-done = s32[32,1,16]{2,1,0:T(1,128)S(1)} async-done(((s32[32,1,16]{2,1,0:T(1,128)}), s32[32,1,16]{2,1,0:T(1,128)S(1)}, u32[]{:S(2)}, u32[]{:S(2)}) %all-to-all-start) | async-done | bytes 2080 | tf_op jit(solution)/shard_map/all_to_all | solution.py:359
  15.2 0.1 reshape_reshape.7.codes_ref
  15.3 1.8 %serve.1 = f32[1024,128]{1,0:T(8,128)} custom-call(s32[512]{0:T(512)S(1)} %reshape_reshape.7.codes_ref, f32[1040,128]{1,0:T(8,128)S(1)} %seen_table.1.table_ref), custom_call_target="tpu_custom_call" | custom-call | tf_op jit(solution)/shard_map/serve/pallas_call | solution.py:159
  17.1 3.0 %all-to-all-start.1 = ((f32[32,32,128]{2,1,0:T(8,128)}), f32[32,32,128]{2,1,0:T(8,128)S(1)}, u32[]{:S(2)}, u32[]{:S(2)}) async-start(f32[32,32,128]{2,1,0:T(8,128)} %bitcast.5), calls=%async_computation.1 | async-start | bytes 1048576 | tf_op jit(solution)/shard_map/all_to_all | solution.py:359
  20.0 0.0 copy-done.5
  20.1 0.1 reshape.31.connect_ref
  20.2 0.1 reshape.28.place_ref
  20.3 2.8 %pixel_sums.1.sums_ref = f32[1152,384]{1,0:T(8,128)S(1)} custom-call(bf16[16,128,128]{2,1,0:T(8,128)(2,1)S(1)} %copy-done.3, bf16[512,384]{1,0:T(8,128)(2,1)S(1)} %copy-done.4), custom_call_target="tpu_custom_call" | custom-call | flops 1811939328 | bytes 1048576 | tf_op jit(solution)/shard_map/pixel_sums/pallas_call | solution.py:86
  23.1 12.4 %all-to-all-done.1 = f32[32,32,128]{2,1,0:T(8,128)S(1)} async-done(((f32[32,32,128]{2,1,0:T(8,128)}), f32[32,32,128]{2,1,0:T(8,128)S(1)}, u32[]{:S(2)}, u32[]{:S(2)}) %all-to-all-start.1) | async-done | bytes 524320 | tf_op jit(solution)/shard_map/all_to_all | solution.py:359
  35.5 7.2 %tile_forces.1 = f32[1024,128]{1,0:T(8,128)} custom-call(s32[256]{0:T(256)S(1)} %reshape.28.place_ref, f32[1024,128]{1,0:T(8,128)S(1)} %bitcast.13, f32[1152,384]{1,0:T(8,128)S(1)} %pixel_sums.1.sums_ref, s32[16,4,8,128]{3,2,1,0:T(8,128)S(1)} %reshape.31.connect_ref), custom_call_target="tpu_custom_call" | custom-call | tf_op jit(solution)/shard_map/tile_forces/pallas_call | solution.py:275
  42.7 3.1 %all-to-all-start.2 = ((f32[32,32,128]{2,1,0:T(8,128)}), f32[32,32,128]{2,1,0:T(8,128)S(1)}, u32[]{:S(2)}, u32[]{:S(2)}) async-start(f32[32,32,128]{2,1,0:T(8,128)} %bitcast.7), calls=%async_computation.2 | async-start | bytes 1048576 | tf_op jit(solution)/shard_map/all_to_all | solution.py:359
  45.9 0.5 broadcast.5
  46.4 0.7 %reduce.5 = s32[32,16]{1,0:T(8,128)S(1)} reduce(s32[32,1,16]{2,1,0:T(1,128)S(1)} %all-to-all-done, s32[]{:T(128)} %broadcast.5), dimensions={1}, to_apply=%all_to_all.9.reduce_sub_computation.5 | reduce | bytes 4100 | tf_op jit(solution)/shard_map/all_to_all | solution.py:359
  47.1 0.1 reshape_reshape.6.codes_ref
  47.1 0.1 hot_table.1
  47.3 13.9 %all-to-all-done.2 = f32[32,32,128]{2,1,0:T(8,128)S(1)} async-done(((f32[32,32,128]{2,1,0:T(8,128)}), f32[32,32,128]{2,1,0:T(8,128)S(1)}, u32[]{:S(2)}, u32[]{:S(2)}) %all-to-all-start.2) | async-done | bytes 524320 | tf_op jit(solution)/shard_map/all_to_all | solution.py:359
  61.1 0.1 broadcast_in_dim.14.calibration_ref
  61.2 1.1 %finish.1 = f32[3,128,128]{2,1,0:T(8,128)} custom-call(f32[24,128]{1,0:T(8,128)S(1)} %broadcast_in_dim.14.calibration_ref, bf16[512,512]{1,0:T(8,128)(2,1)S(1)} %get-tuple-element.7.hot_ref, f32[1024,128]{1,0:T(8,128)S(1)} %bitcast.12, f32[3,128,128]{2,1,0:T(8,128)S(1)} %get-tuple-element.8.damped_ref), custom_call_target="tpu_custom_call" | custom-call | tf_op jit(solution)/shard_map/finish/pallas_call | solution.py:347
  (13 shorter events, 0.0 us)
Async XLA Ops:
  0.0 20.2 %copy-start.6 = (s32[16,16]{1,0:T(8,128)S(1)}, s32[16,16]{1,0:T(8,128)}, u32[]{:S(2)}) copy-start(s32[16,16]{1,0:T(8,128)} %owners_ref.1) | copy-start | bytes 3076
  1.5 13.7 %all-to-all-start = ((s32[32,1,16]{2,1,0:T(1,128)}), s32[32,1,16]{2,1,0:T(1,128)S(1)}, u32[]{:S(2)}, u32[]{:S(2)}) async-start(s32[32,1,16]{2,1,0:T(1,128)} %bitcast.18), calls=%async_computation | async-start | bytes 32768 | tf_op jit(solution)/shard_map/all_to_all | solution.py:359
  9.4 0.9 %copy-start = (f32[128,3,128]{2,0,1:T(8,128)S(1)}, f32[128,3,128]{2,0,1:T(8,128)}, u32[]{:S(2)}) copy-start(f32[128,3,128]{2,0,1:T(8,128)} %param.10) | copy-start | bytes 589828
  10.4 9.7 %copy-start.5 = (s32[16,4,1024]{2,1,0:T(4,128)S(1)}, s32[16,4,1024]{2,1,0:T(4,128)}, u32[]{:S(2)}) copy-start(s32[16,4,1024]{2,1,0:T(4,128)} %param.16) | copy-start | bytes 786436
  10.4 9.9 %copy-start.3 = (bf16[16,128,128]{2,1,0:T(8,128)(2,1)S(1)}, bf16[16,128,128]{2,1,0:T(8,128)(2,1)}, u32[]{:S(2)}) copy-start(bf16[16,128,128]{2,1,0:T(8,128)(2,1)} %images_ref.1) | copy-start | bytes 1572868
  10.4 9.9 %copy-start.4 = (bf16[512,384]{1,0:T(8,128)(2,1)S(1)}, bf16[512,384]{1,0:T(8,128)(2,1)}, u32[]{:S(2)}) copy-start(bf16[512,384]{1,0:T(8,128)(2,1)} %constant.4.clone.pool_ref) | copy-start | bytes 1179652
  17.1 18.4 %all-to-all-start.1 = ((f32[32,32,128]{2,1,0:T(8,128)}), f32[32,32,128]{2,1,0:T(8,128)S(1)}, u32[]{:S(2)}, u32[]{:S(2)}) async-start(f32[32,32,128]{2,1,0:T(8,128)} %bitcast.5), calls=%async_computation.1 | async-start | bytes 1048576 | tf_op jit(solution)/shard_map/all_to_all | solution.py:359
  35.5 11.7 %copy-start.1 = (f32[128,3,128]{2,0,1:T(8,128)S(1)}, f32[128,3,128]{2,0,1:T(8,128)}, u32[]{:S(2)}) copy-start(f32[128,3,128]{2,0,1:T(8,128)} %param.10) | copy-start | bytes 589828
  35.5 11.7 %copy-start.2 = (f32[128,3,128]{2,0,1:T(8,128)S(1)}, f32[128,3,128]{2,0,1:T(8,128)}, u32[]{:S(2)}) copy-start(f32[128,3,128]{2,0,1:T(8,128)} %param.11) | copy-start | bytes 589828
  42.7 18.4 %all-to-all-start.2 = ((f32[32,32,128]{2,1,0:T(8,128)}), f32[32,32,128]{2,1,0:T(8,128)S(1)}, u32[]{:S(2)}, u32[]{:S(2)}) async-start(f32[32,32,128]{2,1,0:T(8,128)} %bitcast.7), calls=%async_computation.2 | async-start | bytes 1048576 | tf_op jit(solution)/shard_map/all_to_all | solution.py:359

commit v4 on v3

--- a/solution.py
+++ b/solution.py
@@ -106,22 +106,21 @@
 
 def table_kernel(calibration_ref, direction_ref, out_ref):
     blocks = direction_ref.shape[1]
-    cameras = calibration_ref.shape[0] // 6
+    cameras = calibration_ref.shape[2]
     half = cameras * blocks
     parts = [direction_ref[axis] for axis in range(3)]
     for camera in range(cameras):
         for motion in range(2):
-            base = camera * 6 + motion * 3
-            seen = calibration_ref[base] * parts[0]
-            seen = seen + calibration_ref[base + 1] * parts[1]
-            seen = seen + calibration_ref[base + 2] * parts[2]
+            seen = calibration_ref[0, motion, camera] * parts[0]
+            seen = seen + calibration_ref[1, motion, camera] * parts[1]
+            seen = seen + calibration_ref[2, motion, camera] * parts[2]
             out_ref[pl.ds(motion * half + camera * blocks, blocks), :] = seen
     out_ref[pl.ds(2 * half, 2 * SUBS), :] = jnp.zeros((2 * SUBS, out_ref.shape[1]), jnp.float32)
 
 
 def seen_table(calibration, direction):
     _, blocks, width = direction.shape
-    cameras = calibration.shape[0] // 6
+    cameras = calibration.shape[2]
     return pl.pallas_call(
         table_kernel,
         in_specs=[pl.BlockSpec(memory_space=pltpu.SMEM), pl.BlockSpec(memory_space=pltpu.VMEM)],
@@ -228,29 +227,44 @@
                 parts[pl.ds(row, SUBS), :] = high
                 parts[pl.ds(row + SUBS, SUBS), :] = total - high
 
-        node_ids = lax.broadcasted_iota(jnp.int32, (LANES, LANES), 0)
+        node_ids = lax.broadcasted_iota(jnp.int32, (LANES, LANES), 0).astype(jnp.float32).astype(jnp.bfloat16)
+        one, zero = jnp.ones((), jnp.bfloat16), jnp.zeros((), jnp.bfloat16)
         block_ids = lax.broadcasted_iota(jnp.int32, (listed, LANES), 0)
-        total = None
+        wide = []
+        picks = []
         for corner in range(4):
             hots = []
             spreads = []
             for chunk in range(SUBS):
                 link = connect_ref[tile, corner, pl.ds(chunk, 1), :]
-                nodes = jnp.broadcast_to(jnp.bitwise_and(link, LANES - 1), (LANES, LANES))
-                hots.append(jnp.where(nodes == node_ids, 1.0, 0.0).astype(jnp.bfloat16))
+                nodes = jnp.bitwise_and(link, LANES - 1).astype(jnp.float32)
+                nodes = jnp.broadcast_to(nodes, (2 * SUBS, LANES)).astype(jnp.bfloat16)
+                hots.append(
+                    jnp.concatenate(
+                        [
+                            jnp.where(nodes == node_ids[row : row + 2 * SUBS], one, zero)
+                            for row in range(0, LANES, 2 * SUBS)
+                        ],
+                        axis=0,
+                    )
+                )
                 here = jnp.broadcast_to(jnp.right_shift(link, 7), (listed, LANES)) == block_ids
                 chosen = []
                 for part in range(4):
                     row = parts[pl.ds((corner * 4 + part) * SUBS + chunk, 1), :]
                     chosen.append(jnp.where(here, jnp.broadcast_to(row, (listed, LANES)), 0.0).astype(jnp.bfloat16))
                 spreads.append(jnp.concatenate(chosen, axis=0))
-            term = lax.dot_general(
-                jnp.concatenate(spreads, axis=1),
-                jnp.concatenate(hots, axis=1),
-                (((1,), (1,)), ((), ())),
-                preferred_element_type=jnp.float32,
-            )
-            total = term if total is None else total + term
+            wide.append(jnp.concatenate(spreads, axis=1))
+            picks.append(jnp.concatenate(hots, axis=1))
+        both = [None, None]
+        for pair in range(2):
+            right = jnp.concatenate(wide[2 * pair : 2 * pair + 2], axis=0)
+            for side in range(2):
+                term = lax.dot_general(
+                    picks[2 * pair + side], right, (((1,), (1,)), ((), ())), preferred_element_type=jnp.float32
+                )
+                both[side] = term if both[side] is None else both[side] + term
+        total = both[0].T[: 4 * listed] + both[1].T[4 * listed :]
         for axis in range(2):
             base = 2 * axis * listed
             result[pl.ds(axis * listed, listed), :] = (
@@ -367,7 +381,6 @@
     capacity = max(2, min(tiles, 4 * tiles * listed // devices))
     direction = direction.transpose(1, 0, 2)
     damping = damping.transpose(1, 0, 2)
-    calibration = calibration.reshape(-1)
     if capacity == tiles:
         wanted = requests(owners, local_block, camera, blocks, devices, cameras * blocks)
         slot = jnp.broadcast_to(jnp.arange(tiles, dtype=jnp.int32)[:, None], owners.shape)
@@ -385,7 +398,7 @@
         slot = jnp.sum(jnp.where(hits, rank[:, :, None], 0), axis=0)
     places = owners * (2 * capacity) + slot
     asked = exchange(wanted.reshape(devices, 1, capacity)).reshape(devices, capacity)
-    table = seen_table(calibration, direction)
+    table = seen_table(calibration.transpose(2, 1, 0), direction)
     sums = pixel_sums(images)
     outgoing = serve(asked, table)
     shape = (devices, 2 * capacity, width)
@@ -393,7 +406,7 @@
     hot, damped = hot_table(asked.reshape(-1, LANES), direction, damping, cameras)
     forces = tile_forces(places, arrived, sums, connect.reshape(tiles, 4, SUBS, LANES), capacity)
     back = exchange(forces.reshape(shape)).reshape(-1, width)
-    product = finish(calibration, hot, back, damped, capacity, devices)
+    product = finish(calibration.reshape(-1), hot, back, damped, capacity, devices)
     return product.transpose(1, 0, 2)
 
 

time: 62.8 us -> 61.8 us (0.984)
  Pallas kernels: 15.2 us -> 14.3 us
    pallas_call x1, Pallas kernels: 7.24 us -> 6.27 us  [tile_forces(): pl.pallas_call(functools.partial(tile_kernel, capacity=capacity, listed=l...]
    unnamed x15 -> x19, local copies, waits for them, and re-layouts: 1.73 us -> 1.73 us
  transfers between devices with their start and end apart: 3 -> 3, of which waited for: 3 -> 3; matrix products, arithmetic and copies ran while one was open for 4% -> 3% of each run, Pallas kernels for 6% -> 6%
where the time goes in v4:
time: 61.8 us; the launch traced here: 61.4 us
  waiting for transfers between devices  30.4 us (49%)
  Pallas kernels  14.3 us (23%)
  starting transfers between devices  13.2 us (21%)
  local copies, waits for them, and re-layouts  2.75 us (4%)
  other arithmetic  0.69 us (1%)
    all_to_all x3, waiting for transfers between devices, exchange(): return lax.all_to_all(values, AXES, split_axis=0, concat_axis=0, tiled=True)  30.4 us
    all_to_all x3, starting transfers between devices, exchange(): return lax.all_to_all(values, AXES, split_axis=0, concat_axis=0, tiled=True)  13.2 us
    pallas_call x1, Pallas kernels, tile_forces(): pl.pallas_call(functools.partial(tile_kernel, capacity=capacity, listed=l...  6.27 us
    pallas_call x1, Pallas kernels, pixel_sums(): pl.pallas_call(functools.partial(pixel_kernel, tiles_step=tiles_step, gro...  2.77 us
    pallas_call x1, Pallas kernels, serve(): pl.pallas_call(functools.partial(serve_kernel, capacity=capacity), in_spe...  1.81 us
    unnamed x19, local copies, waits for them, and re-layouts  1.73 us
    pallas_call x1, Pallas kernels, requests(): pl.pallas_call(functools.partial(request_kernel, blocks=blocks, nothing=n...  1.47 us
  transfers between devices with their start and end apart: 3, of which 3 were waited for; matrix products, arithmetic and copies ran while one was open for 3% of the time, Pallas kernels for 6%

profile of v4, /device:TPU:1, one launch (start us, length us, event | category | flops | bytes accessed | tf_op | source)
XLA Modules:
  0.0 61.4 jit_solution(4208993900193711286)
XLA Ops:
  0.0 1.5 %requests.1 = s32[32,16]{1,0:T(8,128)} custom-call(s32[16,16]{1,0:T(8,128)} %owners_ref.1, s32[16,16]{1,0:T(8,128)} %local_ref.1, s32[1,16]{1,0:T(1,128)} %bitcast.21), custom_call_target="tpu_custom_call" | custom-call | tf_op jit(solution)/shard_map/requests/pallas_call | solution.py:183
  1.5 7.1 %all-to-all-start = ((s32[32,1,16]{2,1,0:T(1,128)}), s32[32,1,16]{2,1,0:T(1,128)S(1)}, u32[]{:S(2)}, u32[]{:S(2)}) async-start(s32[32,1,16]{2,1,0:T(1,128)} %bitcast.20), calls=%async_computation | async-start | bytes 32768 | tf_op jit(solution)/shard_map/all_to_all | solution.py:373
  8.6 0.9 %copy-done = f32[128,3,128]{2,0,1:T(8,128)S(1)} copy-done((f32[128,3,128]{2,0,1:T(8,128)S(1)}, f32[128,3,128]{2,0,1:T(8,128)}, u32[]{:S(2)}) %copy-start) | copy-done | bytes 196632
  9.5 0.7 %copy-done.3 = f32[4,2,3]{0,1,2:T(2,128)S(1)} copy-done((f32[4,2,3]{0,1,2:T(2,128)S(1)}, f32[4,2,3]{0,1,2:T(2,128)}, u32[]{:S(2)}) %copy-start.3) | copy-done | bytes 120
  10.2 0.7 %seen_table.1.table_ref = f32[1040,128]{1,0:T(8,128)S(1)} custom-call(f32[3,2,4]{2,1,0:T(2,128)S(1)} %bitcast.18, f32[3,128,128]{2,1,0:T(8,128)S(1)} %bitcast.15), custom_call_target="tpu_custom_call" | custom-call | flops 1000000 | bytes 98304 | tf_op jit(solution)/shard_map/seen_table/pallas_call | solution.py:124
  10.9 4.3 %all-to-all-done = s32[32,1,16]{2,1,0:T(1,128)S(1)} async-done(((s32[32,1,16]{2,1,0:T(1,128)}), s32[32,1,16]{2,1,0:T(1,128)S(1)}, u32[]{:S(2)}, u32[]{:S(2)}) %all-to-all-start) | async-done | bytes 2080 | tf_op jit(solution)/shard_map/all_to_all | solution.py:373
  15.2 0.1 reshape_reshape.7.codes_ref
  15.3 1.8 %serve.1 = f32[1024,128]{1,0:T(8,128)} custom-call(s32[512]{0:T(512)S(1)} %reshape_reshape.7.codes_ref, f32[1040,128]{1,0:T(8,128)S(1)} %seen_table.1.table_ref), custom_call_target="tpu_custom_call" | custom-call | tf_op jit(solution)/shard_map/serve/pallas_call | solution.py:158
  17.1 3.0 %all-to-all-start.1 = ((f32[32,32,128]{2,1,0:T(8,128)}), f32[32,32,128]{2,1,0:T(8,128)S(1)}, u32[]{:S(2)}, u32[]{:S(2)}) async-start(f32[32,32,128]{2,1,0:T(8,128)} %bitcast.6), calls=%async_computation.1 | async-start | bytes 1048576 | tf_op jit(solution)/shard_map/all_to_all | solution.py:373
  20.1 0.1 reshape.30.connect_ref
  20.2 0.1 reshape.27.place_ref
  20.3 2.8 %pixel_sums.1.sums_ref = f32[1152,384]{1,0:T(8,128)S(1)} custom-call(bf16[16,128,128]{2,1,0:T(8,128)(2,1)S(1)} %copy-done.5, bf16[512,384]{1,0:T(8,128)(2,1)S(1)} %copy-done.6), custom_call_target="tpu_custom_call" | custom-call | flops 1811939328 | bytes 1048576 | tf_op jit(solution)/shard_map/pixel_sums/pallas_call | solution.py:86
  23.1 12.4 %all-to-all-done.1 = f32[32,32,128]{2,1,0:T(8,128)S(1)} async-done(((f32[32,32,128]{2,1,0:T(8,128)}), f32[32,32,128]{2,1,0:T(8,128)S(1)}, u32[]{:S(2)}, u32[]{:S(2)}) %all-to-all-start.1) | async-done | bytes 524320 | tf_op jit(solution)/shard_map/all_to_all | solution.py:373
  35.5 6.3 %tile_forces.1 = f32[1024,128]{1,0:T(8,128)} custom-call(s32[256]{0:T(256)S(1)} %reshape.27.place_ref, f32[1024,128]{1,0:T(8,128)S(1)} %bitcast.14, f32[1152,384]{1,0:T(8,128)S(1)} %pixel_sums.1.sums_ref, s32[16,4,8,128]{3,2,1,0:T(8,128)S(1)} %reshape.30.connect_ref), custom_call_target="tpu_custom_call" | custom-call | tf_op jit(solution)/shard_map/tile_forces/pallas_call | solution.py:289
  41.8 3.1 %all-to-all-start.2 = ((f32[32,32,128]{2,1,0:T(8,128)}), f32[32,32,128]{2,1,0:T(8,128)S(1)}, u32[]{:S(2)}, u32[]{:S(2)}) async-start(f32[32,32,128]{2,1,0:T(8,128)} %bitcast.8), calls=%async_computation.2 | async-start | bytes 1048576 | tf_op jit(solution)/shard_map/all_to_all | solution.py:373
  44.9 0.1 copy.12
  45.0 0.1 broadcast_in_dim.6
  45.1 0.5 broadcast.5
  45.6 0.7 %reduce.5 = s32[32,16]{1,0:T(8,128)S(1)} reduce(s32[32,1,16]{2,1,0:T(1,128)S(1)} %all-to-all-done, s32[]{:T(128)} %broadcast.5), dimensions={1}, to_apply=%all_to_all.9.reduce_sub_computation.5 | reduce | bytes 4100 | tf_op jit(solution)/shard_map/all_to_all | solution.py:373
  46.3 0.1 reshape_reshape.6.codes_ref
  46.4 0.1 hot_table.1
  46.5 13.7 %all-to-all-done.2 = f32[32,32,128]{2,1,0:T(8,128)S(1)} async-done(((f32[32,32,128]{2,1,0:T(8,128)}), f32[32,32,128]{2,1,0:T(8,128)S(1)}, u32[]{:S(2)}, u32[]{:S(2)}) %all-to-all-start.2) | async-done | bytes 524320 | tf_op jit(solution)/shard_map/all_to_all | solution.py:373
  60.2 0.1 broadcast_in_dim.14.calibration_ref
  60.3 1.1 %finish.1 = f32[3,128,128]{2,1,0:T(8,128)} custom-call(f32[24,128]{1,0:T(8,128)S(1)} %broadcast_in_dim.14.calibration_ref, bf16[512,512]{1,0:T(8,128)(2,1)S(1)} %get-tuple-element.7.hot_ref, f32[1024,128]{1,0:T(8,128)S(1)} %bitcast.13, f32[3,128,128]{2,1,0:T(8,128)S(1)} %get-tuple-element.8.damped_ref), custom_call_target="tpu_custom_call" | custom-call | tf_op jit(solution)/shard_map/finish/pallas_call | solution.py:361
  (17 shorter events, 0.0 us)
Async XLA Ops:
  0.0 20.2 %copy-start.8 = (s32[16,16]{1,0:T(8,128)S(1)}, s32[16,16]{1,0:T(8,128)}, u32[]{:S(2)}) copy-start(s32[16,16]{1,0:T(8,128)} %owners_ref.1) | copy-start | bytes 3076
  1.5 13.7 %all-to-all-start = ((s32[32,1,16]{2,1,0:T(1,128)}), s32[32,1,16]{2,1,0:T(1,128)S(1)}, u32[]{:S(2)}, u32[]{:S(2)}) async-start(s32[32,1,16]{2,1,0:T(1,128)} %bitcast.20), calls=%async_computation | async-start | bytes 32768 | tf_op jit(solution)/shard_map/all_to_all | solution.py:373
  8.6 0.9 %copy-start = (f32[128,3,128]{2,0,1:T(8,128)S(1)}, f32[128,3,128]{2,0,1:T(8,128)}, u32[]{:S(2)}) copy-start(f32[128,3,128]{2,0,1:T(8,128)} %param.10) | copy-start | bytes 589828
  9.5 0.7 %copy-start.3 = (f32[4,2,3]{0,1,2:T(2,128)S(1)}, f32[4,2,3]{0,1,2:T(2,128)}, u32[]{:S(2)}) copy-start(f32[4,2,3]{0,1,2:T(2,128)} %param.12) | copy-start | bytes 292
  10.2 9.9 %copy-start.7 = (s32[16,4,1024]{2,1,0:T(4,128)S(1)}, s32[16,4,1024]{2,1,0:T(4,128)}, u32[]{:S(2)}) copy-start(s32[16,4,1024]{2,1,0:T(4,128)} %param.16) | copy-start | bytes 786436
  10.2 10.1 %copy-start.5 = (bf16[16,128,128]{2,1,0:T(8,128)(2,1)S(1)}, bf16[16,128,128]{2,1,0:T(8,128)(2,1)}, u32[]{:S(2)}) copy-start(bf16[16,128,128]{2,1,0:T(8,128)(2,1)} %images_ref.1) | copy-start | bytes 1572868
  10.2 10.1 %copy-start.6 = (bf16[512,384]{1,0:T(8,128)(2,1)S(1)}, bf16[512,384]{1,0:T(8,128)(2,1)}, u32[]{:S(2)}) copy-start(bf16[512,384]{1,0:T(8,128)(2,1)} %constant.4.clone.pool_ref) | copy-start | bytes 1179652
  17.1 18.4 %all-to-all-start.1 = ((f32[32,32,128]{2,1,0:T(8,128)}), f32[32,32,128]{2,1,0:T(8,128)S(1)}, u32[]{:S(2)}, u32[]{:S(2)}) async-start(f32[32,32,128]{2,1,0:T(8,128)} %bitcast.6), calls=%async_computation.1 | async-start | bytes 1048576 | tf_op jit(solution)/shard_map/all_to_all | solution.py:373
  35.5 9.4 %copy-start.4 = (f32[4,2,3]{0,1,2:T(2,128)S(1)}, f32[4,2,3]{0,1,2:T(2,128)}, u32[]{:S(2)}) copy-start(f32[4,2,3]{0,1,2:T(2,128)} %param.12) | copy-start | bytes 292
  35.5 10.9 %copy-start.1 = (f32[128,3,128]{2,0,1:T(8,128)S(1)}, f32[128,3,128]{2,0,1:T(8,128)}, u32[]{:S(2)}) copy-start(f32[128,3,128]{2,0,1:T(8,128)} %param.10) | copy-start | bytes 589828
  35.5 10.9 %copy-start.2 = (f32[128,3,128]{2,0,1:T(8,128)S(1)}, f32[128,3,128]{2,0,1:T(8,128)}, u32[]{:S(2)}) copy-start(f32[128,3,128]{2,0,1:T(8,128)} %param.11) | copy-start | bytes 589828
  41.8 18.4 %all-to-all-start.2 = ((f32[32,32,128]{2,1,0:T(8,128)}), f32[32,32,128]{2,1,0:T(8,128)S(1)}, u32[]{:S(2)}, u32[]{:S(2)}) async-start(f32[32,32,128]{2,1,0:T(8,128)} %bitcast.8), calls=%async_computation.2 | async-start | bytes 1048576 | tf_op jit(solution)/shard_map/all_to_all | solution.py:373

commit v5 on v4

--- a/solution.py
+++ b/solution.py
@@ -229,7 +229,7 @@
 
         node_ids = lax.broadcasted_iota(jnp.int32, (LANES, LANES), 0).astype(jnp.float32).astype(jnp.bfloat16)
         one, zero = jnp.ones((), jnp.bfloat16), jnp.zeros((), jnp.bfloat16)
-        block_ids = lax.broadcasted_iota(jnp.int32, (listed, LANES), 0)
+        block_ids = lax.broadcasted_iota(jnp.int32, (listed, LANES), 0).astype(jnp.float32).astype(jnp.bfloat16)
         wide = []
         picks = []
         for corner in range(4):
@@ -248,11 +248,12 @@
                         axis=0,
                     )
                 )
-                here = jnp.broadcast_to(jnp.right_shift(link, 7), (listed, LANES)) == block_ids
+                block = jnp.right_shift(link, 7).astype(jnp.float32)
+                here = jnp.broadcast_to(block, (listed, LANES)).astype(jnp.bfloat16) == block_ids
                 chosen = []
                 for part in range(4):
                     row = parts[pl.ds((corner * 4 + part) * SUBS + chunk, 1), :]
-                    chosen.append(jnp.where(here, jnp.broadcast_to(row, (listed, LANES)), 0.0).astype(jnp.bfloat16))
+                    chosen.append(jnp.where(here, jnp.broadcast_to(row, (listed, LANES)).astype(jnp.bfloat16), zero))
                 spreads.append(jnp.concatenate(chosen, axis=0))
             wide.append(jnp.concatenate(spreads, axis=1))
             picks.append(jnp.concatenate(hots, axis=1))

time: 61.8 us -> 61.8 us (level)
  no operation moved by 1% of the time
where the time goes in v5:
time: 61.8 us; the launch traced here: 61.4 us
  waiting for transfers between devices  30.4 us (49%)
  Pallas kernels  14.3 us (23%)
  starting transfers between devices  13.2 us (21%)
  local copies, waits for them, and re-layouts  2.75 us (4%)
  other arithmetic  0.69 us (1%)
    all_to_all x3, waiting for transfers between devices, exchange(): return lax.all_to_all(values, AXES, split_axis=0, concat_axis=0, tiled=True)  30.4 us
    all_to_all x3, starting transfers between devices, exchange(): return lax.all_to_all(values, AXES, split_axis=0, concat_axis=0, tiled=True)  13.2 us
    pallas_call x1, Pallas kernels, tile_forces(): pl.pallas_call(functools.partial(tile_kernel, capacity=capacity, listed=l...  6.3 us
    pallas_call x1, Pallas kernels, pixel_sums(): pl.pallas_call(functools.partial(pixel_kernel, tiles_step=tiles_step, gro...  2.77 us
    pallas_call x1, Pallas kernels, serve(): pl.pallas_call(functools.partial(serve_kernel, capacity=capacity), in_spe...  1.81 us
    unnamed x19, local copies, waits for them, and re-layouts  1.73 us
    pallas_call x1, Pallas kernels, requests(): pl.pallas_call(functools.partial(request_kernel, blocks=blocks, nothing=n...  1.47 us
  transfers between devices with their start and end apart: 3, of which 3 were waited for; matrix products, arithmetic and copies ran while one was open for 3% of the time, Pallas kernels for 6%

profile of v5, /device:TPU:1, one launch (start us, length us, event | category | flops | bytes accessed | tf_op | source)
XLA Modules:
  0.0 61.4 jit_solution(14340522526012980130)
XLA Ops:
  0.0 1.5 %requests.1 = s32[32,16]{1,0:T(8,128)} custom-call(s32[16,16]{1,0:T(8,128)} %owners_ref.1, s32[16,16]{1,0:T(8,128)} %local_ref.1, s32[1,16]{1,0:T(1,128)} %bitcast.21), custom_call_target="tpu_custom_call" | custom-call | tf_op jit(solution)/shard_map/requests/pallas_call | solution.py:183
  1.5 7.1 %all-to-all-start = ((s32[32,1,16]{2,1,0:T(1,128)}), s32[32,1,16]{2,1,0:T(1,128)S(1)}, u32[]{:S(2)}, u32[]{:S(2)}) async-start(s32[32,1,16]{2,1,0:T(1,128)} %bitcast.20), calls=%async_computation | async-start | bytes 32768 | tf_op jit(solution)/shard_map/all_to_all | solution.py:374
  8.6 0.9 %copy-done = f32[128,3,128]{2,0,1:T(8,128)S(1)} copy-done((f32[128,3,128]{2,0,1:T(8,128)S(1)}, f32[128,3,128]{2,0,1:T(8,128)}, u32[]{:S(2)}) %copy-start) | copy-done | bytes 196632
  9.5 0.7 %copy-done.3 = f32[4,2,3]{0,1,2:T(2,128)S(1)} copy-done((f32[4,2,3]{0,1,2:T(2,128)S(1)}, f32[4,2,3]{0,1,2:T(2,128)}, u32[]{:S(2)}) %copy-start.3) | copy-done | bytes 120
  10.2 0.7 %seen_table.1.table_ref = f32[1040,128]{1,0:T(8,128)S(1)} custom-call(f32[3,2,4]{2,1,0:T(2,128)S(1)} %bitcast.18, f32[3,128,128]{2,1,0:T(8,128)S(1)} %bitcast.15), custom_call_target="tpu_custom_call" | custom-call | flops 1000000 | bytes 98304 | tf_op jit(solution)/shard_map/seen_table/pallas_call | solution.py:124
  10.9 4.3 %all-to-all-done = s32[32,1,16]{2,1,0:T(1,128)S(1)} async-done(((s32[32,1,16]{2,1,0:T(1,128)}), s32[32,1,16]{2,1,0:T(1,128)S(1)}, u32[]{:S(2)}, u32[]{:S(2)}) %all-to-all-start) | async-done | bytes 2080 | tf_op jit(solution)/shard_map/all_to_all | solution.py:374
  15.2 0.1 reshape_reshape.7.codes_ref
  15.3 1.8 %serve.1 = f32[1024,128]{1,0:T(8,128)} custom-call(s32[512]{0:T(512)S(1)} %reshape_reshape.7.codes_ref, f32[1040,128]{1,0:T(8,128)S(1)} %seen_table.1.table_ref), custom_call_target="tpu_custom_call" | custom-call | tf_op jit(solution)/shard_map/serve/pallas_call | solution.py:158
  17.1 3.0 %all-to-all-start.1 = ((f32[32,32,128]{2,1,0:T(8,128)}), f32[32,32,128]{2,1,0:T(8,128)S(1)}, u32[]{:S(2)}, u32[]{:S(2)}) async-start(f32[32,32,128]{2,1,0:T(8,128)} %bitcast.6), calls=%async_computation.1 | async-start | bytes 1048576 | tf_op jit(solution)/shard_map/all_to_all | solution.py:374
  20.1 0.1 reshape.30.connect_ref
  20.2 0.1 reshape.27.place_ref
  20.3 2.8 %pixel_sums.1.sums_ref = f32[1152,384]{1,0:T(8,128)S(1)} custom-call(bf16[16,128,128]{2,1,0:T(8,128)(2,1)S(1)} %copy-done.5, bf16[512,384]{1,0:T(8,128)(2,1)S(1)} %copy-done.6), custom_call_target="tpu_custom_call" | custom-call | flops 1811939328 | bytes 1048576 | tf_op jit(solution)/shard_map/pixel_sums/pallas_call | solution.py:86
  23.1 12.4 %all-to-all-done.1 = f32[32,32,128]{2,1,0:T(8,128)S(1)} async-done(((f32[32,32,128]{2,1,0:T(8,128)}), f32[32,32,128]{2,1,0:T(8,128)S(1)}, u32[]{:S(2)}, u32[]{:S(2)}) %all-to-all-start.1) | async-done | bytes 524320 | tf_op jit(solution)/shard_map/all_to_all | solution.py:374
  35.5 6.3 %tile_forces.1 = f32[1024,128]{1,0:T(8,128)} custom-call(s32[256]{0:T(256)S(1)} %reshape.27.place_ref, f32[1024,128]{1,0:T(8,128)S(1)} %bitcast.14, f32[1152,384]{1,0:T(8,128)S(1)} %pixel_sums.1.sums_ref, s32[16,4,8,128]{3,2,1,0:T(8,128)S(1)} %reshape.30.connect_ref), custom_call_target="tpu_custom_call" | custom-call | tf_op jit(solution)/shard_map/tile_forces/pallas_call | solution.py:290
  41.8 3.1 %all-to-all-start.2 = ((f32[32,32,128]{2,1,0:T(8,128)}), f32[32,32,128]{2,1,0:T(8,128)S(1)}, u32[]{:S(2)}, u32[]{:S(2)}) async-start(f32[32,32,128]{2,1,0:T(8,128)} %bitcast.8), calls=%async_computation.2 | async-start | bytes 1048576 | tf_op jit(solution)/shard_map/all_to_all | solution.py:374
  44.9 0.1 copy.12
  45.0 0.1 broadcast_in_dim.6
  45.1 0.5 broadcast.5
  45.6 0.7 %reduce.5 = s32[32,16]{1,0:T(8,128)S(1)} reduce(s32[32,1,16]{2,1,0:T(1,128)S(1)} %all-to-all-done, s32[]{:T(128)} %broadcast.5), dimensions={1}, to_apply=%all_to_all.9.reduce_sub_computation.5 | reduce | bytes 4100 | tf_op jit(solution)/shard_map/all_to_all | solution.py:374
  46.3 0.1 reshape_reshape.6.codes_ref
  46.4 0.1 hot_table.1
  46.6 13.7 %all-to-all-done.2 = f32[32,32,128]{2,1,0:T(8,128)S(1)} async-done(((f32[32,32,128]{2,1,0:T(8,128)}), f32[32,32,128]{2,1,0:T(8,128)S(1)}, u32[]{:S(2)}, u32[]{:S(2)}) %all-to-all-start.2) | async-done | bytes 524320 | tf_op jit(solution)/shard_map/all_to_all | solution.py:374
  60.2 0.1 broadcast_in_dim.14.calibration_ref
  60.3 1.1 %finish.1 = f32[3,128,128]{2,1,0:T(8,128)} custom-call(f32[24,128]{1,0:T(8,128)S(1)} %broadcast_in_dim.14.calibration_ref, bf16[512,512]{1,0:T(8,128)(2,1)S(1)} %get-tuple-element.7.hot_ref, f32[1024,128]{1,0:T(8,128)S(1)} %bitcast.13, f32[3,128,128]{2,1,0:T(8,128)S(1)} %get-tuple-element.8.damped_ref), custom_call_target="tpu_custom_call" | custom-call | tf_op jit(solution)/shard_map/finish/pallas_call | solution.py:362
  (17 shorter events, 0.0 us)
Async XLA Ops:
  0.0 20.2 %copy-start.8 = (s32[16,16]{1,0:T(8,128)S(1)}, s32[16,16]{1,0:T(8,128)}, u32[]{:S(2)}) copy-start(s32[16,16]{1,0:T(8,128)} %owners_ref.1) | copy-start | bytes 3076
  1.5 13.7 %all-to-all-start = ((s32[32,1,16]{2,1,0:T(1,128)}), s32[32,1,16]{2,1,0:T(1,128)S(1)}, u32[]{:S(2)}, u32[]{:S(2)}) async-start(s32[32,1,16]{2,1,0:T(1,128)} %bitcast.20), calls=%async_computation | async-start | bytes 32768 | tf_op jit(solution)/shard_map/all_to_all | solution.py:374
  8.6 0.9 %copy-start = (f32[128,3,128]{2,0,1:T(8,128)S(1)}, f32[128,3,128]{2,0,1:T(8,128)}, u32[]{:S(2)}) copy-start(f32[128,3,128]{2,0,1:T(8,128)} %param.10) | copy-start | bytes 589828
  9.5 0.7 %copy-start.3 = (f32[4,2,3]{0,1,2:T(2,128)S(1)}, f32[4,2,3]{0,1,2:T(2,128)}, u32[]{:S(2)}) copy-start(f32[4,2,3]{0,1,2:T(2,128)} %param.12) | copy-start | bytes 292
  10.2 9.9 %copy-start.7 = (s32[16,4,1024]{2,1,0:T(4,128)S(1)}, s32[16,4,1024]{2,1,0:T(4,128)}, u32[]{:S(2)}) copy-start(s32[16,4,1024]{2,1,0:T(4,128)} %param.16) | copy-start | bytes 786436
  10.2 10.1 %copy-start.5 = (bf16[16,128,128]{2,1,0:T(8,128)(2,1)S(1)}, bf16[16,128,128]{2,1,0:T(8,128)(2,1)}, u32[]{:S(2)}) copy-start(bf16[16,128,128]{2,1,0:T(8,128)(2,1)} %images_ref.1) | copy-start | bytes 1572868
  10.2 10.1 %copy-start.6 = (bf16[512,384]{1,0:T(8,128)(2,1)S(1)}, bf16[512,384]{1,0:T(8,128)(2,1)}, u32[]{:S(2)}) copy-start(bf16[512,384]{1,0:T(8,128)(2,1)} %constant.4.clone.pool_ref) | copy-start | bytes 1179652
  17.1 18.4 %all-to-all-start.1 = ((f32[32,32,128]{2,1,0:T(8,128)}), f32[32,32,128]{2,1,0:T(8,128)S(1)}, u32[]{:S(2)}, u32[]{:S(2)}) async-start(f32[32,32,128]{2,1,0:T(8,128)} %bitcast.6), calls=%async_computation.1 | async-start | bytes 1048576 | tf_op jit(solution)/shard_map/all_to_all | solution.py:374
  35.5 9.4 %copy-start.4 = (f32[4,2,3]{0,1,2:T(2,128)S(1)}, f32[4,2,3]{0,1,2:T(2,128)}, u32[]{:S(2)}) copy-start(f32[4,2,3]{0,1,2:T(2,128)} %param.12) | copy-start | bytes 292
  35.5 10.9 %copy-start.1 = (f32[128,3,128]{2,0,1:T(8,128)S(1)}, f32[128,3,128]{2,0,1:T(8,128)}, u32[]{:S(2)}) copy-start(f32[128,3,128]{2,0,1:T(8,128)} %param.10) | copy-start | bytes 589828
  35.5 10.9 %copy-start.2 = (f32[128,3,128]{2,0,1:T(8,128)S(1)}, f32[128,3,128]{2,0,1:T(8,128)}, u32[]{:S(2)}) copy-start(f32[128,3,128]{2,0,1:T(8,128)} %param.11) | copy-start | bytes 589828
  41.8 18.4 %all-to-all-start.2 = ((f32[32,32,128]{2,1,0:T(8,128)}), f32[32,32,128]{2,1,0:T(8,128)S(1)}, u32[]{:S(2)}, u32[]{:S(2)}) async-start(f32[32,32,128]{2,1,0:T(8,128)} %bitcast.8), calls=%async_computation.2 | async-start | bytes 1048576 | tf_op jit(solution)/shard_map/all_to_all | solution.py:374

commit v6 on v4

--- a/solution.py
+++ b/solution.py
@@ -160,7 +160,7 @@
         in_specs=[pl.BlockSpec(memory_space=pltpu.SMEM), pl.BlockSpec(memory_space=pltpu.VMEM)],
         out_specs=pl.BlockSpec(memory_space=pl.ANY),
         out_shape=jax.ShapeDtypeStruct(shape, jnp.float32),
-        scratch_shapes=[pltpu.VMEM(shape, jnp.float32), pltpu.SemaphoreType.DMA((math.gcd(devices, 8),))],
+        scratch_shapes=[pltpu.VMEM(shape, jnp.float32), pltpu.SemaphoreType.DMA((math.gcd(devices, 4),))],
         compiler_params=pltpu.CompilerParams(vmem_limit_bytes=VMEM_LIMIT),
         name="serve",
     )(codes.reshape(-1), table)

time: 61.8 us -> 61.8 us (level)
  no operation moved by 1% of the time
where the time goes in v6:
time: 61.8 us; the launch traced here: 61.4 us
  waiting for transfers between devices  30.4 us (49%)
  Pallas kernels  14.3 us (23%)
  starting transfers between devices  13.2 us (21%)
  local copies, waits for them, and re-layouts  2.75 us (4%)
  other arithmetic  0.69 us (1%)
    all_to_all x3, waiting for transfers between devices, exchange(): return lax.all_to_all(values, AXES, split_axis=0, concat_axis=0, tiled=True)  30.4 us
    all_to_all x3, starting transfers between devices, exchange(): return lax.all_to_all(values, AXES, split_axis=0, concat_axis=0, tiled=True)  13.2 us
    pallas_call x1, Pallas kernels, tile_forces(): pl.pallas_call(functools.partial(tile_kernel, capacity=capacity, listed=l...  6.27 us
    pallas_call x1, Pallas kernels, pixel_sums(): pl.pallas_call(functools.partial(pixel_kernel, tiles_step=tiles_step, gro...  2.78 us
    pallas_call x1, Pallas kernels, serve(): pl.pallas_call(functools.partial(serve_kernel, capacity=capacity), in_spe...  1.79 us
    unnamed x19, local copies, waits for them, and re-layouts  1.73 us
    pallas_call x1, Pallas kernels, requests(): pl.pallas_call(functools.partial(request_kernel, blocks=blocks, nothing=n...  1.47 us
  transfers between devices with their start and end apart: 3, of which 3 were waited for; matrix products, arithmetic and copies ran while one was open for 3% of the time, Pallas kernels for 6%

profile of v6, /device:TPU:1, one launch (start us, length us, event | category | flops | bytes accessed | tf_op | source)
XLA Modules:
  0.0 61.4 jit_solution(16919984028504862984)
XLA Ops:
  0.0 1.5 %requests.1 = s32[32,16]{1,0:T(8,128)} custom-call(s32[16,16]{1,0:T(8,128)} %owners_ref.1, s32[16,16]{1,0:T(8,128)} %local_ref.1, s32[1,16]{1,0:T(1,128)} %bitcast.21), custom_call_target="tpu_custom_call" | custom-call | tf_op jit(solution)/shard_map/requests/pallas_call | solution.py:183
  1.5 7.1 %all-to-all-start = ((s32[32,1,16]{2,1,0:T(1,128)}), s32[32,1,16]{2,1,0:T(1,128)S(1)}, u32[]{:S(2)}, u32[]{:S(2)}) async-start(s32[32,1,16]{2,1,0:T(1,128)} %bitcast.20), calls=%async_computation | async-start | bytes 32768 | tf_op jit(solution)/shard_map/all_to_all | solution.py:373
  8.6 0.9 %copy-done = f32[128,3,128]{2,0,1:T(8,128)S(1)} copy-done((f32[128,3,128]{2,0,1:T(8,128)S(1)}, f32[128,3,128]{2,0,1:T(8,128)}, u32[]{:S(2)}) %copy-start) | copy-done | bytes 196632
  9.5 0.7 %copy-done.3 = f32[4,2,3]{0,1,2:T(2,128)S(1)} copy-done((f32[4,2,3]{0,1,2:T(2,128)S(1)}, f32[4,2,3]{0,1,2:T(2,128)}, u32[]{:S(2)}) %copy-start.3) | copy-done | bytes 120
  10.2 0.7 %seen_table.1.table_ref = f32[1040,128]{1,0:T(8,128)S(1)} custom-call(f32[3,2,4]{2,1,0:T(2,128)S(1)} %bitcast.18, f32[3,128,128]{2,1,0:T(8,128)S(1)} %bitcast.15), custom_call_target="tpu_custom_call" | custom-call | flops 1000000 | bytes 98304 | tf_op jit(solution)/shard_map/seen_table/pallas_call | solution.py:124
  10.9 4.3 %all-to-all-done = s32[32,1,16]{2,1,0:T(1,128)S(1)} async-done(((s32[32,1,16]{2,1,0:T(1,128)}), s32[32,1,16]{2,1,0:T(1,128)S(1)}, u32[]{:S(2)}, u32[]{:S(2)}) %all-to-all-start) | async-done | bytes 2080 | tf_op jit(solution)/shard_map/all_to_all | solution.py:373
  15.2 0.1 reshape_reshape.7.codes_ref
  15.3 1.8 %serve.1 = f32[1024,128]{1,0:T(8,128)} custom-call(s32[512]{0:T(512)S(1)} %reshape_reshape.7.codes_ref, f32[1040,128]{1,0:T(8,128)S(1)} %seen_table.1.table_ref), custom_call_target="tpu_custom_call" | custom-call | tf_op jit(solution)/shard_map/serve/pallas_call | solution.py:158
  17.1 3.0 %all-to-all-start.1 = ((f32[32,32,128]{2,1,0:T(8,128)}), f32[32,32,128]{2,1,0:T(8,128)S(1)}, u32[]{:S(2)}, u32[]{:S(2)}) async-start(f32[32,32,128]{2,1,0:T(8,128)} %bitcast.6), calls=%async_computation.1 | async-start | bytes 1048576 | tf_op jit(solution)/shard_map/all_to_all | solution.py:373
  20.1 0.1 reshape.30.connect_ref
  20.2 0.1 reshape.27.place_ref
  20.3 2.8 %pixel_sums.1.sums_ref = f32[1152,384]{1,0:T(8,128)S(1)} custom-call(bf16[16,128,128]{2,1,0:T(8,128)(2,1)S(1)} %copy-done.5, bf16[512,384]{1,0:T(8,128)(2,1)S(1)} %copy-done.6), custom_call_target="tpu_custom_call" | custom-call | flops 1811939328 | bytes 1048576 | tf_op jit(solution)/shard_map/pixel_sums/pallas_call | solution.py:86
  23.1 12.4 %all-to-all-done.1 = f32[32,32,128]{2,1,0:T(8,128)S(1)} async-done(((f32[32,32,128]{2,1,0:T(8,128)}), f32[32,32,128]{2,1,0:T(8,128)S(1)}, u32[]{:S(2)}, u32[]{:S(2)}) %all-to-all-start.1) | async-done | bytes 524320 | tf_op jit(solution)/shard_map/all_to_all | solution.py:373
  35.5 6.3 %tile_forces.1 = f32[1024,128]{1,0:T(8,128)} custom-call(s32[256]{0:T(256)S(1)} %reshape.27.place_ref, f32[1024,128]{1,0:T(8,128)S(1)} %bitcast.14, f32[1152,384]{1,0:T(8,128)S(1)} %pixel_sums.1.sums_ref, s32[16,4,8,128]{3,2,1,0:T(8,128)S(1)} %reshape.30.connect_ref), custom_call_target="tpu_custom_call" | custom-call | tf_op jit(solution)/shard_map/tile_forces/pallas_call | solution.py:289
  41.8 3.1 %all-to-all-start.2 = ((f32[32,32,128]{2,1,0:T(8,128)}), f32[32,32,128]{2,1,0:T(8,128)S(1)}, u32[]{:S(2)}, u32[]{:S(2)}) async-start(f32[32,32,128]{2,1,0:T(8,128)} %bitcast.8), calls=%async_computation.2 | async-start | bytes 1048576 | tf_op jit(solution)/shard_map/all_to_all | solution.py:373
  44.9 0.1 copy.12
  45.0 0.1 broadcast_in_dim.6
  45.1 0.5 broadcast.5
  45.6 0.7 %reduce.5 = s32[32,16]{1,0:T(8,128)S(1)} reduce(s32[32,1,16]{2,1,0:T(1,128)S(1)} %all-to-all-done, s32[]{:T(128)} %broadcast.5), dimensions={1}, to_apply=%all_to_all.9.reduce_sub_computation.5 | reduce | bytes 4100 | tf_op jit(solution)/shard_map/all_to_all | solution.py:373
  46.3 0.1 reshape_reshape.6.codes_ref
  46.4 0.1 hot_table.1
  46.5 13.7 %all-to-all-done.2 = f32[32,32,128]{2,1,0:T(8,128)S(1)} async-done(((f32[32,32,128]{2,1,0:T(8,128)}), f32[32,32,128]{2,1,0:T(8,128)S(1)}, u32[]{:S(2)}, u32[]{:S(2)}) %all-to-all-start.2) | async-done | bytes 524320 | tf_op jit(solution)/shard_map/all_to_all | solution.py:373
  60.2 0.1 broadcast_in_dim.14.calibration_ref
  60.3 1.1 %finish.1 = f32[3,128,128]{2,1,0:T(8,128)} custom-call(f32[24,128]{1,0:T(8,128)S(1)} %broadcast_in_dim.14.calibration_ref, bf16[512,512]{1,0:T(8,128)(2,1)S(1)} %get-tuple-element.7.hot_ref, f32[1024,128]{1,0:T(8,128)S(1)} %bitcast.13, f32[3,128,128]{2,1,0:T(8,128)S(1)} %get-tuple-element.8.damped_ref), custom_call_target="tpu_custom_call" | custom-call | tf_op jit(solution)/shard_map/finish/pallas_call | solution.py:361
  (17 shorter events, 0.0 us)
Async XLA Ops:
  0.0 20.2 %copy-start.8 = (s32[16,16]{1,0:T(8,128)S(1)}, s32[16,16]{1,0:T(8,128)}, u32[]{:S(2)}) copy-start(s32[16,16]{1,0:T(8,128)} %owners_ref.1) | copy-start | bytes 3076
  1.5 13.7 %all-to-all-start = ((s32[32,1,16]{2,1,0:T(1,128)}), s32[32,1,16]{2,1,0:T(1,128)S(1)}, u32[]{:S(2)}, u32[]{:S(2)}) async-start(s32[32,1,16]{2,1,0:T(1,128)} %bitcast.20), calls=%async_computation | async-start | bytes 32768 | tf_op jit(solution)/shard_map/all_to_all | solution.py:373
  8.6 0.9 %copy-start = (f32[128,3,128]{2,0,1:T(8,128)S(1)}, f32[128,3,128]{2,0,1:T(8,128)}, u32[]{:S(2)}) copy-start(f32[128,3,128]{2,0,1:T(8,128)} %param.10) | copy-start | bytes 589828
  9.5 0.7 %copy-start.3 = (f32[4,2,3]{0,1,2:T(2,128)S(1)}, f32[4,2,3]{0,1,2:T(2,128)}, u32[]{:S(2)}) copy-start(f32[4,2,3]{0,1,2:T(2,128)} %param.12) | copy-start | bytes 292
  10.2 9.9 %copy-start.7 = (s32[16,4,1024]{2,1,0:T(4,128)S(1)}, s32[16,4,1024]{2,1,0:T(4,128)}, u32[]{:S(2)}) copy-start(s32[16,4,1024]{2,1,0:T(4,128)} %param.16) | copy-start | bytes 786436
  10.2 10.1 %copy-start.5 = (bf16[16,128,128]{2,1,0:T(8,128)(2,1)S(1)}, bf16[16,128,128]{2,1,0:T(8,128)(2,1)}, u32[]{:S(2)}) copy-start(bf16[16,128,128]{2,1,0:T(8,128)(2,1)} %images_ref.1) | copy-start | bytes 1572868
  10.2 10.1 %copy-start.6 = (bf16[512,384]{1,0:T(8,128)(2,1)S(1)}, bf16[512,384]{1,0:T(8,128)(2,1)}, u32[]{:S(2)}) copy-start(bf16[512,384]{1,0:T(8,128)(2,1)} %constant.4.clone.pool_ref) | copy-start | bytes 1179652
  17.1 18.4 %all-to-all-start.1 = ((f32[32,32,128]{2,1,0:T(8,128)}), f32[32,32,128]{2,1,0:T(8,128)S(1)}, u32[]{:S(2)}, u32[]{:S(2)}) async-start(f32[32,32,128]{2,1,0:T(8,128)} %bitcast.6), calls=%async_computation.1 | async-start | bytes 1048576 | tf_op jit(solution)/shard_map/all_to_all | solution.py:373
  35.5 9.4 %copy-start.4 = (f32[4,2,3]{0,1,2:T(2,128)S(1)}, f32[4,2,3]{0,1,2:T(2,128)}, u32[]{:S(2)}) copy-start(f32[4,2,3]{0,1,2:T(2,128)} %param.12) | copy-start | bytes 292
  35.5 10.9 %copy-start.1 = (f32[128,3,128]{2,0,1:T(8,128)S(1)}, f32[128,3,128]{2,0,1:T(8,128)}, u32[]{:S(2)}) copy-start(f32[128,3,128]{2,0,1:T(8,128)} %param.10) | copy-start | bytes 589828
  35.5 10.9 %copy-start.2 = (f32[128,3,128]{2,0,1:T(8,128)S(1)}, f32[128,3,128]{2,0,1:T(8,128)}, u32[]{:S(2)}) copy-start(f32[128,3,128]{2,0,1:T(8,128)} %param.11) | copy-start | bytes 589828
  41.8 18.4 %all-to-all-start.2 = ((f32[32,32,128]{2,1,0:T(8,128)}), f32[32,32,128]{2,1,0:T(8,128)S(1)}, u32[]{:S(2)}, u32[]{:S(2)}) async-start(f32[32,32,128]{2,1,0:T(8,128)} %bitcast.8), calls=%async_computation.2 | async-start | bytes 1048576 | tf_op jit(solution)/shard_map/all_to_all | solution.py:373
